TPU v7x, 32 devices: a whole 2x2x4 slice. The times are simulated.
32 devices in a mesh: batch: 4 (over x, core), ctx: 8 (over z, y).
Axes of the slice: x: 2, y: 2, z: 4, core: 2. Of those that a mesh axis runs over, the one named last changes fastest.
Arguments:
- hidden_in: bfloat16 [4096, 1536], P(('batch', 'ctx')), may hold values from -6 to 6
- positions: int32 [4096], P(('batch', 'ctx')), may hold values from 0 to 1023, as said below
- doc_ids: int32 [4096], P(('batch', 'ctx')), may hold values from 0 to 2, as said below
- attn_gain: bfloat16 [1536], P(('batch', 'ctx')), may hold values from 0.25 to 1.75
- q_weight: bfloat16 [1536, 1536], P(('batch', 'ctx')), may hold values from -0.15625 to 0.15625
- q_bias: bfloat16 [1536], P(('batch', 'ctx')), may hold values from -3 to 3
- k_weight: bfloat16 [1536, 256], P(('batch', 'ctx')), may hold values from -0.15625 to 0.15625
- k_bias: bfloat16 [256], P(('batch', 'ctx')), may hold values from -3 to 3
- v_weight: bfloat16 [1536, 256], P(('batch', 'ctx')), may hold values from -0.15625 to 0.15625
- v_bias: bfloat16 [256], P(('batch', 'ctx')), may hold values from -3 to 3
- o_weight: bfloat16 [1536, 1536], P(('batch', 'ctx')), may hold values from -1.25 to 1.25
- mlp_gain: bfloat16 [1536], P(('batch', 'ctx')), may hold values from 0.25 to 1.75
- gate_weight: bfloat16 [1536, 8960], P(('batch', 'ctx')), may hold values from -0.15625 to 0.15625
- up_weight: bfloat16 [1536, 8960], P(('batch', 'ctx')), may hold values from -0.15625 to 0.15625
- down_weight: bfloat16 [8960, 1536], P(('batch', 'ctx')), may hold values from -0.0625 to 0.0625
- out_grad: bfloat16 [4096, 1536], P(('batch', 'ctx')), may hold values from -6 to 6
Outputs:
- hidden_out: bfloat16 [4096, 1536], P(('batch', 'ctx'))
- hidden_grad: float32 [4096, 1536], P(('batch', 'ctx'))
- attn_gain_grad: float32 [1536], P(('batch', 'ctx'))
- q_weight_grad: float32 [1536, 1536], P(('batch', 'ctx'))
- q_bias_grad: float32 [1536], P(('batch', 'ctx'))
- k_weight_grad: float32 [1536, 256], P(('batch', 'ctx'))
- k_bias_grad: float32 [256], P(('batch', 'ctx'))
- v_weight_grad: float32 [1536, 256], P(('batch', 'ctx'))
- v_bias_grad: float32 [256], P(('batch', 'ctx'))
- o_weight_grad: float32 [1536, 1536], P(('batch', 'ctx'))
- mlp_gain_grad: float32 [1536], P(('batch', 'ctx'))
- gate_weight_grad: float32 [1536, 8960], P(('batch', 'ctx'))
- up_weight_grad: float32 [1536, 8960], P(('batch', 'ctx'))
- down_weight_grad: float32 [8960, 1536], P(('batch', 'ctx'))
Inputs may be any that keep to these rules, and one draw needn't show every extreme that they name: Each device's 128 rows are 1 runs of 128 rows, run s holding tokens of sequence s of its batch index; within a batch index every position of each sequence is held exactly once. On ctx index c a run holds either positions c * 128 onward in order, or block c and then block 15 - c of 64 positions each, in order. `doc_ids`: never falls as the position within a sequence rises; each of a sequence's three documents holds 128 positions or more.
All inputs are finite; a program needn't handle non-finite values.
Results may differ from a plain program's by a relative error of at most 0.015.
Values may be sent and summed in bfloat16 or wider, within the bound.
A program may use at most 448 MiB of HBM per device.

v0:
```python
import math

import jax
import jax.numpy as jnp
from jax import lax
from jax.sharding import PartitionSpec as P

HEADS = 12
KV_HEADS = 2
HEAD_DIM = 128
SEQS = 1


EPSILON = 1e-06
ROPE_BASE = 10000.0
MASKED = -1e30


def rope_tables(positions):
    half_dim = HEAD_DIM // 2
    inverse_freq = jnp.exp(
        jnp.arange(half_dim, dtype=jnp.float32) * (-2.0 * math.log(ROPE_BASE) / HEAD_DIM)
    )
    angles = positions.astype(jnp.float32)[:, None] * inverse_freq[None, :]
    angles = jnp.concatenate([angles, angles], axis=1)
    return (jnp.cos(angles), jnp.sin(angles))


def rotate(values, cosine, sine_table):
    half_dim = values.shape[-1] // 2
    turned = jnp.concatenate([-values[..., half_dim:], values[..., :half_dim]], axis=-1)
    return values * cosine[:, None, :] + turned * sine_table[:, None, :]


def rotate_back(grad_rows, cosine, sine_table):
    half_dim = grad_rows.shape[-1] // 2
    scaled = grad_rows * sine_table[:, None, :]
    turned = jnp.concatenate([scaled[..., half_dim:], -scaled[..., :half_dim]], axis=-1)
    return grad_rows * cosine[:, None, :] + turned


def norm_rows(values, gain_vector):
    factor = lax.rsqrt(jnp.mean(values * values, axis=-1, keepdims=True) + EPSILON)
    return (values * factor * gain_vector, factor)


def norm_back(values, factor, gain_vector, grad_rows):
    scaled = grad_rows * gain_vector
    gain_grad = jnp.sum(grad_rows * values * factor, axis=0)
    value_grad = factor * scaled - values * (factor * factor * factor) * jnp.mean(
        scaled * values, axis=-1, keepdims=True
    )
    return (value_grad, gain_grad)


def contract_rows(lhs_matrix, rhs_matrix):
    return lax.dot_general(
        lhs_matrix, rhs_matrix, (((0,), (0,)), ((), ())), preferred_element_type=jnp.float32
    )


def times_transposed(lhs_matrix, rhs_matrix):
    return lax.dot_general(
        lhs_matrix, rhs_matrix, (((1,), (1,)), ((), ())), preferred_element_type=jnp.float32
    )


def key_mask(query_pos, query_doc, key_pos, key_doc):
    pos_here = key_pos.transpose(1, 0, 2)
    doc_here = key_doc.transpose(1, 0, 2)
    return (pos_here[:, None] <= query_pos[:, :, None, None]) & (
        doc_here[:, None] == query_doc[:, :, None, None]
    )


def block_scores(query_heads, key_block, allowed):
    scores = jnp.einsum(
        "sqjhd,gstjd->sjhqgt", query_heads, key_block, preferred_element_type=jnp.float32
    ) * HEAD_DIM ** (-0.5)
    scores = jnp.where(allowed[:, None, None], scores, MASKED)
    return scores.reshape(scores.shape[:4] + (-1,))


def unflatten(scores, key_block):
    return scores.reshape(scores.shape[:4] + (key_block.shape[0], key_block.shape[2]))


def attend(query_heads, query_pos, query_doc, key_blocks, value_blocks, pos_blocks, doc_blocks):
    seqs_here, query_len, kv_heads, groups, head_dim = query_heads.shape
    stat_shape = (seqs_here, kv_heads, groups, query_len)

    def stats_step(state, inputs):
        key_block, key_pos, key_doc = inputs
        allowed = key_mask(query_pos, query_doc, key_pos, key_doc)
        running_max, row_total = state
        scores = block_scores(query_heads, key_block, allowed)
        new_max = jnp.maximum(running_max, jnp.max(scores, axis=-1))
        row_total = row_total * jnp.exp(running_max - new_max) + jnp.sum(
            jnp.exp(scores - new_max[..., None]), axis=-1
        )
        state = (new_max, row_total)
        return (state, None)

    start_state = (jnp.full(stat_shape, MASKED, jnp.float32), jnp.zeros(stat_shape, jnp.float32))
    (running_max, row_total), unused = lax.scan(
        stats_step, start_state, (key_blocks, pos_blocks, doc_blocks)
    )
    log_total = running_max + jnp.log(row_total)

    def value_step(summed, inputs):
        key_block, value_block, key_pos, key_doc = inputs
        allowed = key_mask(query_pos, query_doc, key_pos, key_doc)
        scores = block_scores(query_heads, key_block, allowed)
        attn_probs = unflatten(
            jnp.exp(scores - log_total[..., None]).astype(jnp.bfloat16), key_block
        )
        summed = summed + jnp.einsum(
            "sjhqgt,gstjd->sjhqd", attn_probs, value_block, preferred_element_type=jnp.float32
        )
        return (summed, None)

    start_sum = jnp.zeros(stat_shape + (head_dim,), jnp.float32)
    summed, unused = lax.scan(
        value_step, start_sum, (key_blocks, value_blocks, pos_blocks, doc_blocks)
    )
    result = summed.transpose(0, 3, 1, 2, 4).reshape(
        seqs_here * query_len, kv_heads * groups * head_dim
    )
    return (result, log_total)


def attend_back(
    query_heads,
    query_pos,
    query_doc,
    key_blocks,
    value_blocks,
    pos_blocks,
    doc_blocks,
    log_total,
    grad_heads,
):
    seqs_here, query_len, kv_heads, groups, head_dim = query_heads.shape
    stat_shape = (seqs_here, kv_heads, groups, query_len)

    def delta_step(row_delta, inputs):
        key_block, value_block, key_pos, key_doc = inputs
        allowed = key_mask(query_pos, query_doc, key_pos, key_doc)
        scores = block_scores(query_heads, key_block, allowed)
        attn_probs = jnp.exp(scores - log_total[..., None])
        grad_probs = jnp.einsum(
            "sqjhd,gstjd->sjhqgt", grad_heads, value_block, preferred_element_type=jnp.float32
        )
        row_delta = row_delta + jnp.sum(attn_probs * grad_probs.reshape(attn_probs.shape), axis=-1)
        return (row_delta, None)

    inputs_all = (key_blocks, value_blocks, pos_blocks, doc_blocks)
    row_delta, unused = lax.scan(delta_step, jnp.zeros(stat_shape, jnp.float32), inputs_all)

    def grad_step(grad_query, inputs):
        key_block, value_block, key_pos, key_doc = inputs
        allowed = key_mask(query_pos, query_doc, key_pos, key_doc)
        scores = block_scores(query_heads, key_block, allowed)
        attn_probs = jnp.exp(scores - log_total[..., None])
        grad_probs = jnp.einsum(
            "sqjhd,gstjd->sjhqgt", grad_heads, value_block, preferred_element_type=jnp.float32
        )
        grad_scores = unflatten(
            (attn_probs * (grad_probs.reshape(attn_probs.shape) - row_delta[..., None])).astype(
                jnp.bfloat16
            ),
            key_block,
        )
        probs_low = unflatten(attn_probs.astype(jnp.bfloat16), key_block)
        new_query = grad_query + jnp.einsum(
            "sjhqgt,gstjd->sqjhd", grad_scores, key_block, preferred_element_type=jnp.float32
        )
        grad_key = jnp.einsum(
            "sjhqgt,sqjhd->gstjd", grad_scores, query_heads, preferred_element_type=jnp.float32
        )
        grad_value = jnp.einsum(
            "sjhqgt,sqjhd->gstjd", probs_low, grad_heads, preferred_element_type=jnp.float32
        )
        return (new_query, (grad_key, grad_value))

    start_query = jnp.zeros(query_heads.shape, jnp.float32)
    grad_query, (key_grads, value_grads) = lax.scan(grad_step, start_query, inputs_all)
    inv_root = HEAD_DIM ** (-0.5)
    kv_width = kv_heads * head_dim
    return (
        grad_query * inv_root,
        key_grads.reshape(-1, kv_width) * inv_root,
        value_grads.reshape(-1, kv_width),
    )


def gather_attention(gain_vector, w_query, b_query, w_key, b_key, w_value, b_value, w_out):
    return (
        lax.all_gather(gain_vector, ("batch", "ctx"), axis=0, tiled=True),
        lax.all_gather(w_query, ("batch", "ctx"), axis=0, tiled=True),
        lax.all_gather(b_query, ("batch", "ctx"), axis=0, tiled=True),
        lax.all_gather(w_key, ("batch", "ctx"), axis=0, tiled=True),
        lax.all_gather(b_key, ("batch", "ctx"), axis=0, tiled=True),
        lax.all_gather(w_value, ("batch", "ctx"), axis=0, tiled=True),
        lax.all_gather(b_value, ("batch", "ctx"), axis=0, tiled=True),
        lax.all_gather(w_out, ("batch", "ctx"), axis=0, tiled=True),
    )


def gather_mlp(gain_vector, w_gate, w_up, w_down):
    return (
        lax.all_gather(gain_vector, ("batch", "ctx"), axis=0, tiled=True),
        lax.all_gather(w_gate, ("batch", "ctx"), axis=0, tiled=True),
        lax.all_gather(w_up, ("batch", "ctx"), axis=0, tiled=True),
        lax.all_gather(w_down, ("batch", "ctx"), axis=0, tiled=True),
    )


def own_slice(vector):
    owners = lax.axis_size(("batch", "ctx"))
    width = vector.shape[0] // owners
    return lax.dynamic_slice_in_dim(vector, lax.axis_index(("batch", "ctx")) * width, width)


def local(
    hidden_in,
    positions,
    doc_ids,
    attn_gain,
    q_weight,
    q_bias,
    k_weight,
    k_bias,
    v_weight,
    v_bias,
    o_weight,
    mlp_gain,
    gate_weight,
    up_weight,
    down_weight,
    out_grad,
):
    row_count = hidden_in.shape[0]
    query_len = row_count // SEQS
    groups = HEADS // KV_HEADS
    kv_width = KV_HEADS * HEAD_DIM
    cosine, sine_table = rope_tables(positions)
    query_pos = positions.reshape(SEQS, query_len)
    query_doc = doc_ids.reshape(SEQS, query_len)
    gain_one, w_query, b_query, w_key, b_key, w_value, b_value, w_out = gather_attention(
        attn_gain, q_weight, q_bias, k_weight, k_bias, v_weight, v_bias, o_weight
    )
    hidden_wide = hidden_in.astype(jnp.float32)
    normed_wide, factor_one = norm_rows(hidden_wide, gain_one.astype(jnp.float32))
    normed_one = normed_wide.astype(jnp.bfloat16)
    q_lin = jnp.dot(normed_one, w_query, preferred_element_type=jnp.float32) + b_query.astype(
        jnp.float32
    )
    k_lin = jnp.dot(normed_one, w_key, preferred_element_type=jnp.float32) + b_key.astype(
        jnp.float32
    )
    v_lin = jnp.dot(normed_one, w_value, preferred_element_type=jnp.float32) + b_value.astype(
        jnp.float32
    )
    queries = rotate(q_lin.reshape(row_count, HEADS, HEAD_DIM), cosine, sine_table).astype(
        jnp.bfloat16
    )
    key_rows = (
        rotate(k_lin.reshape(row_count, KV_HEADS, HEAD_DIM), cosine, sine_table)
        .astype(jnp.bfloat16)
        .reshape(row_count, kv_width)
    )
    value_rows = v_lin.astype(jnp.bfloat16)
    key_all, value_all, pos_all, doc_all = (
        lax.all_gather(key_rows, "ctx", axis=0, tiled=True),
        lax.all_gather(value_rows, "ctx", axis=0, tiled=True),
        lax.all_gather(positions, "ctx", axis=0, tiled=True),
        lax.all_gather(doc_ids, "ctx", axis=0, tiled=True),
    )
    shards = key_all.shape[0] // row_count
    per_block = 4
    block_shape = (shards // per_block, per_block, SEQS, query_len)
    key_blocks = key_all.reshape(block_shape + (KV_HEADS, HEAD_DIM))
    value_blocks = value_all.reshape(block_shape + (KV_HEADS, HEAD_DIM))
    pos_blocks = pos_all.reshape(block_shape)
    doc_blocks = doc_all.reshape(block_shape)
    query_heads = queries.reshape(SEQS, query_len, KV_HEADS, groups, HEAD_DIM)
    attn_wide, log_total = attend(
        query_heads, query_pos, query_doc, key_blocks, value_blocks, pos_blocks, doc_blocks
    )
    attn_out = attn_wide.astype(jnp.bfloat16)
    residual = hidden_wide + jnp.dot(attn_out, w_out, preferred_element_type=jnp.float32)
    gain_two, w_gate, w_up, w_down = gather_mlp(mlp_gain, gate_weight, up_weight, down_weight)
    normed_mid, factor_two = norm_rows(residual, gain_two.astype(jnp.float32))
    normed_two = normed_mid.astype(jnp.bfloat16)
    gate_lin = jnp.dot(normed_two, w_gate, preferred_element_type=jnp.float32)
    up_lin = jnp.dot(normed_two, w_up, preferred_element_type=jnp.float32)
    sigmoid_gate = jax.nn.sigmoid(gate_lin)
    mixed_rows = (gate_lin * sigmoid_gate * up_lin).astype(jnp.bfloat16)
    hidden_out = (
        residual + jnp.dot(mixed_rows, w_down, preferred_element_type=jnp.float32)
    ).astype(jnp.bfloat16)
    kept_state = lax.optimization_barrier(
        (
            attn_gain,
            q_weight,
            q_bias,
            k_weight,
            k_bias,
            v_weight,
            v_bias,
            o_weight,
            mlp_gain,
            gate_weight,
            up_weight,
            down_weight,
            hidden_out,
        )
    )
    gain_two, w_gate, w_up, w_down = gather_mlp(
        kept_state[8], kept_state[9], kept_state[10], kept_state[11]
    )
    down_grad = contract_rows(mixed_rows, out_grad)
    d_mixed = times_transposed(out_grad, w_down)
    d_gate = (d_mixed * up_lin * sigmoid_gate * (1.0 + gate_lin * (1.0 - sigmoid_gate))).astype(
        jnp.bfloat16
    )
    d_up = (d_mixed * (gate_lin * sigmoid_gate)).astype(jnp.bfloat16)
    gate_grad = contract_rows(normed_two, d_gate)
    up_grad = contract_rows(normed_two, d_up)
    d_normed_two = times_transposed(d_gate, w_gate) + times_transposed(d_up, w_up)
    d_residual_norm, gain_two_grad = norm_back(
        residual, factor_two, gain_two.astype(jnp.float32), d_normed_two
    )
    d_residual = out_grad.astype(jnp.float32) + d_residual_norm
    gain_one, w_query, b_query, w_key, b_key, w_value, b_value, w_out = gather_attention(
        kept_state[0],
        kept_state[1],
        kept_state[2],
        kept_state[3],
        kept_state[4],
        kept_state[5],
        kept_state[6],
        kept_state[7],
    )
    d_branch = d_residual.astype(jnp.bfloat16)
    out_proj_grad = contract_rows(attn_out, d_branch)
    d_attn = times_transposed(d_branch, w_out).astype(jnp.bfloat16)
    grad_heads = d_attn.reshape(SEQS, query_len, KV_HEADS, groups, HEAD_DIM)
    d_queries, d_keys_all, d_values_all = attend_back(
        query_heads,
        query_pos,
        query_doc,
        key_blocks,
        value_blocks,
        pos_blocks,
        doc_blocks,
        log_total,
        grad_heads,
    )
    d_keys, d_values = (
        lax.psum_scatter(d_keys_all, "ctx", scatter_dimension=0, tiled=True),
        lax.psum_scatter(d_values_all, "ctx", scatter_dimension=0, tiled=True),
    )
    d_q_lin = (
        rotate_back(d_queries.reshape(row_count, HEADS, HEAD_DIM), cosine, sine_table)
        .reshape(row_count, HEADS * HEAD_DIM)
        .astype(jnp.bfloat16)
    )
    d_k_lin = (
        rotate_back(d_keys.reshape(row_count, KV_HEADS, HEAD_DIM), cosine, sine_table)
        .reshape(row_count, kv_width)
        .astype(jnp.bfloat16)
    )
    d_v_lin = d_values.astype(jnp.bfloat16)
    query_grad = contract_rows(normed_one, d_q_lin)
    query_bias_grad = jnp.sum(d_q_lin.astype(jnp.float32), axis=0)
    key_grad = contract_rows(normed_one, d_k_lin)
    key_bias_grad = jnp.sum(d_k_lin.astype(jnp.float32), axis=0)
    value_grad = contract_rows(normed_one, d_v_lin)
    value_bias_grad = jnp.sum(d_v_lin.astype(jnp.float32), axis=0)
    d_normed_one = (
        times_transposed(d_q_lin, w_query)
        + times_transposed(d_k_lin, w_key)
        + times_transposed(d_v_lin, w_value)
    )
    d_hidden_norm, gain_one_grad = norm_back(
        hidden_wide, factor_one, gain_one.astype(jnp.float32), d_normed_one
    )
    hidden_grad = d_residual + d_hidden_norm
    small_sums = lax.psum(
        (gain_one_grad, query_bias_grad, key_bias_grad, value_bias_grad, gain_two_grad),
        ("batch", "ctx"),
    )
    small_own = tuple((own_slice(vector) for vector in small_sums))
    matrix_sums = (
        lax.psum_scatter(query_grad, ("batch", "ctx"), scatter_dimension=0, tiled=True),
        lax.psum_scatter(key_grad, ("batch", "ctx"), scatter_dimension=0, tiled=True),
        lax.psum_scatter(value_grad, ("batch", "ctx"), scatter_dimension=0, tiled=True),
        lax.psum_scatter(out_proj_grad, ("batch", "ctx"), scatter_dimension=0, tiled=True),
        lax.psum_scatter(gate_grad, ("batch", "ctx"), scatter_dimension=0, tiled=True),
        lax.psum_scatter(up_grad, ("batch", "ctx"), scatter_dimension=0, tiled=True),
        lax.psum_scatter(down_grad, ("batch", "ctx"), scatter_dimension=0, tiled=True),
    )
    return (
        hidden_out,
        hidden_grad,
        small_own[0],
        matrix_sums[0],
        small_own[1],
        matrix_sums[1],
        small_own[2],
        matrix_sums[2],
        small_own[3],
        matrix_sums[3],
        small_own[4],
        matrix_sums[4],
        matrix_sums[5],
        matrix_sums[6],
    )


def solution(mesh):
    placed = (
        P(("batch", "ctx"), None),
        P(("batch", "ctx")),
        P(("batch", "ctx")),
        P(("batch", "ctx")),
        P(("batch", "ctx"), None),
        P(("batch", "ctx")),
        P(("batch", "ctx"), None),
        P(("batch", "ctx")),
        P(("batch", "ctx"), None),
        P(("batch", "ctx")),
        P(("batch", "ctx"), None),
        P(("batch", "ctx")),
        P(("batch", "ctx"), None),
        P(("batch", "ctx"), None),
        P(("batch", "ctx"), None),
        P(("batch", "ctx"), None),
    )
    return jax.shard_map(
        local,
        mesh=mesh,
        in_specs=placed,
        out_specs=(
            P(("batch", "ctx"), None),
            P(("batch", "ctx"), None),
            P(("batch", "ctx")),
            P(("batch", "ctx"), None),
            P(("batch", "ctx")),
            P(("batch", "ctx"), None),
            P(("batch", "ctx")),
            P(("batch", "ctx"), None),
            P(("batch", "ctx")),
            P(("batch", "ctx"), None),
            P(("batch", "ctx")),
            P(("batch", "ctx"), None),
            P(("batch", "ctx"), None),
            P(("batch", "ctx"), None),
        ),
        check_vma=False,
    )
```

profile of v0, /device:TPU:0, one launch (start us, length us, event | category | flops | bytes accessed | tf_op | source)
XLA Modules:
  0.0 3378.9 jit_solution(18059051122949944035)
XLA Ops:
  14.9 42.6 %all-reduce.10 = (bf16[256]{0:T(256)(128)(2,1)S(1)}, bf16[1536]{0:T(1024)(128)(2,1)S(1)}, bf16[1536]{0:T(1024)(128)(2,1)S(1)}, bf16[256]{0:T(256)(128)(2,1)S(1)}, bf16[1536]{0:T(1024)(128)(2,1)S(1)}) all-reduce(bf16[256]{0:T(256)(128)(2,1)S(1)} %dynamic-update-slice.1, ...), channel_id=1, replica_groups=mesh['batch'=4,'ctx'=8] {'batch','ctx'}, use_global_device_ids=true, to_apply=%add.1 | all-reduce | flops 5120 | bytes 20480
  58.3 73.0 %all_gather.78 = bf16[1536,256]{1,0:T(8,128)(2,1)S(1)} all-gather(bf16[48,256]{1,0:T(8,128)(2,1)S(1)} %copy-done.38), channel_id=1, replica_groups=mesh['batch'=4,'ctx'=8] {'batch','ctx'}, dimensions={0}, use_global_device_ids=true | all-gather | bytes 811008 | tf_op jit(solution)/shard_map/all_gather | solution.py:202
  134.7 31.9 all_gather.80
  167.6 74.6 %all_gather.83 = bf16[1536,256]{1,0:T(8,128)(2,1)S(1)} all-gather(bf16[48,256]{1,0:T(8,128)(2,1)S(1)} %copy-done.40), channel_id=1, replica_groups=mesh['batch'=4,'ctx'=8] {'batch','ctx'}, dimensions={0}, use_global_device_ids=true | all-gather | bytes 811008 | tf_op jit(solution)/shard_map/all_gather | solution.py:204
  242.5 33.5 all_gather.85
  361.3 138.5 %all-gather.19.cloned.1.call-done = bf16[1536,8960]{1,0:T(8,128)(2,1)} async-done(((bf16[48,8960]{1,0:T(8,128)(2,1)}), bf16[1536,8960]{1,0:T(8,128)(2,1)}) %all-gather.19.cloned.1.call-update) | async-done | bytes 27525136 | tf_op jit(solution)/shard_map/all_gather | solution.py:214
  518.4 148.4 %all-gather.21.cloned.1.call-done = bf16[8960,1536]{1,0:T(8,128)(2,1)} async-done(((bf16[280,1536]{1,0:T(8,128)(2,1)}), bf16[8960,1536]{1,0:T(8,128)(2,1)}) %all-gather.21.cloned.1.call-update) | async-done | bytes 27525136 | tf_op jit(solution)/shard_map/all_gather | solution.py:215
  683.9 39.8 %all-reduce.9 = (bf16[1536]{0:T(1024)(128)(2,1)S(1)}, bf16[1536]{0:T(1024)(128)(2,1)}) all-reduce(bf16[1536]{0:T(1024)(128)(2,1)S(1)} %dynamic-update-slice.5, bf16[1536]{0:T(1024)(128)(2,1)S(1)} %dynamic-update-slice.6), channel_id=1, replica_groups=mesh['batch'=4,'ctx'=8] {'batch','ctx'}, use_global_device_ids=true, to_apply=%add.5 | all-reduce | flops 3072 | bytes 12288
  723.7 123.1 %all-gather.23.cloned.1.call-done = bf16[8960,1536]{1,0:T(8,128)(2,1)} async-done(((bf16[280,1536]{1,0:T(8,128)(2,1)}), bf16[8960,1536]{1,0:T(8,128)(2,1)}) %all-gather.23.cloned.1.call-update) | async-done | bytes 27525136 | tf_op jit(solution)/shard_map/all_gather | solution.py:215
  865.9 148.0 %all-gather.25.cloned.1.call-done = bf16[1536,8960]{1,0:T(8,128)(2,1)} async-done(((bf16[48,8960]{1,0:T(8,128)(2,1)}), bf16[1536,8960]{1,0:T(8,128)(2,1)}) %all-gather.25.cloned.1.call-update) | async-done | bytes 27525136 | tf_op jit(solution)/shard_map/all_gather | solution.py:213
  1028.4 152.5 %all-gather.27.cloned.1.call-done = bf16[1536,8960]{1,0:T(8,128)(2,1)} async-done(((bf16[48,8960]{1,0:T(8,128)(2,1)}), bf16[1536,8960]{1,0:T(8,128)(2,1)}) %all-gather.27.cloned.1.call-update) | async-done | bytes 27525136 | tf_op jit(solution)/shard_map/all_gather | solution.py:214
  1198.4 47.4 %all-gather.29.cloned.1.call-done = bf16[1536,1536]{1,0:T(8,128)(2,1)} async-done(((bf16[48,1536]{1,0:T(8,128)(2,1)}), bf16[1536,1536]{1,0:T(8,128)(2,1)}) %all-gather.29.cloned.1.call-update) | async-done | bytes 4718608 | tf_op jit(solution)/shard_map/all_gather | solution.py:206
  1285.2 60.7 %reduce-scatter.12.cloned.1.call-done = f32[128,256]{1,0:T(8,128)} async-done(((f32[1024,256]{1,0:T(8,128)}), f32[128,256]{1,0:T(8,128)}) %reduce-scatter.12.cloned.1.call-update) | async-done | bytes 131088 | tf_op jit(solution)/shard_map/reduce_scatter | solution.py:362
  1350.2 62.6 %reduce-scatter.14.cloned.1.call-done = f32[128,256]{1,0:T(8,128)} async-done(((f32[1024,256]{1,0:T(8,128)}), f32[128,256]{1,0:T(8,128)}) %reduce-scatter.14.cloned.1.call-update) | async-done | bytes 131088 | tf_op jit(solution)/shard_map/reduce_scatter | solution.py:363
  1452.8 23.5 fusion.125
  1476.4 23.4 fusion.126
  1500.6 75.3 %all_gather.97 = bf16[1536,256]{1,0:T(8,128)(2,1)} all-gather(bf16[48,256]{1,0:T(8,128)(2,1)S(1)} %copy-done.39), channel_id=1, replica_groups=mesh['batch'=4,'ctx'=8] {'batch','ctx'}, dimensions={0}, use_global_device_ids=true | all-gather | bytes 811008 | tf_op jit(solution)/shard_map/all_gather | solution.py:202
  1575.9 74.1 %all_gather.98 = bf16[1536,256]{1,0:T(8,128)(2,1)} all-gather(bf16[48,256]{1,0:T(8,128)(2,1)S(1)} %copy-done.41), channel_id=1, replica_groups=mesh['batch'=4,'ctx'=8] {'batch','ctx'}, dimensions={0}, use_global_device_ids=true | all-gather | bytes 811008 | tf_op jit(solution)/shard_map/all_gather | solution.py:204
  1655.6 38.7 %all-reduce.8 = (f32[1536]{0:T(1024)S(1)}, f32[1536]{0:T(1024)S(1)}, f32[256]{0:T(256)S(1)}, f32[256]{0:T(256)S(1)}, f32[1536]{0:T(1024)S(1)}) all-reduce(f32[1536]{0:T(1024)S(1)} %get-tuple-element.548, f32[1536]{0:T(1024)S(1)} %reduce_sum.111, f32[256]{0:T(256)S(1)} %get-tuple-element.650, ...), channel_id=1, replica_groups=mesh['batch'=4,'ctx'=8] {'batch','ctx'}, use_global_device_ids=true, to_apply=%region_18.19 | all-reduce | flops 5120 | bytes 40960 | tf_op jit(solution)/shard_map/psum | solution.py:391
  1698.5 125.4 %reduce-scatter.16.cloned.1.call-done = f32[48,1536]{1,0:T(8,128)} async-done(((f32[1536,1536]{1,0:T(8,128)}), f32[48,1536]{1,0:T(8,128)}) %reduce-scatter.16.cloned.1.call-update) | async-done | bytes 294928 | tf_op jit(solution)/shard_map/reduce_scatter | solution.py:397
  1823.8 142.2 %reduce-scatter.22.cloned.1.call-done = f32[48,1536]{1,0:T(8,128)} async-done(((f32[1536,1536]{1,0:T(8,128)}), f32[48,1536]{1,0:T(8,128)}) %reduce-scatter.22.cloned.1.call-update) | async-done | bytes 294928 | tf_op jit(solution)/shard_map/reduce_scatter | solution.py:400
  1966.1 468.1 %reduce-scatter.28.cloned.1.call-done = f32[280,1536]{1,0:T(8,128)} async-done(((f32[8960,1536]{1,0:T(8,128)}), f32[280,1536]{1,0:T(8,128)}) %reduce-scatter.28.cloned.1.call-update) | async-done | bytes 1720336
  2434.2 469.3 %reduce-scatter.24.cloned.1.call-done = f32[48,8960]{1,0:T(8,128)} async-done(((f32[1536,8960]{1,0:T(8,128)}), f32[48,8960]{1,0:T(8,128)}) %reduce-scatter.24.cloned.1.call-update) | async-done | bytes 1720336 | tf_op jit(solution)/shard_map/reduce_scatter | solution.py:401
  2903.5 468.4 %reduce-scatter.26.cloned.1.call-done = f32[48,8960]{1,0:T(8,128)} async-done(((f32[1536,8960]{1,0:T(8,128)}), f32[48,8960]{1,0:T(8,128)}) %reduce-scatter.26.cloned.1.call-update) | async-done | bytes 1720336 | tf_op jit(solution)/shard_map/reduce_scatter | solution.py:402
  (314 shorter events, 327.1 us)
Async XLA Ops:
  7.2 307.0 %all-gather.13.cloned.1.call-start = ((), (), s32[]{:S(2)}) async-start(), calls=%async_computation.9 | async-start | bytes 4866048 | tf_op jit(solution)/shard_map/all_gather | solution.py:200
  7.9 334.6 %all-gather.15.cloned.1.call-start = ((), (), s32[]{:S(2)}) async-start(), calls=%async_computation.10 | async-start | bytes 4866048 | tf_op jit(solution)/shard_map/all_gather | solution.py:206
  8.7 337.7 %all-gather.17.cloned.1.call-start = ((), (), s32[]{:S(2)}) async-start(), calls=%async_computation.11 | async-start | bytes 28385280 | tf_op jit(solution)/shard_map/all_gather | solution.py:213
  9.4 490.4 %all-gather.19.cloned.1.call-start = ((), (), s32[]{:S(2)}) async-start(), calls=%async_computation.12 | async-start | bytes 28385280 | tf_op jit(solution)/shard_map/all_gather | solution.py:214
  10.0 656.8 %all-gather.21.cloned.1.call-start = ((), (), s32[]{:S(2)}) async-start(), calls=%async_computation.13 | async-start | bytes 28385280 | tf_op jit(solution)/shard_map/all_gather | solution.py:215
  10.6 836.2 %all-gather.23.cloned.1.call-start = ((), (), s32[]{:S(2)}) async-start(), calls=%async_computation.14 | async-start | bytes 28385280 | tf_op jit(solution)/shard_map/all_gather | solution.py:215
  57.6 256.7 %copy-start.33 = (f32[1536]{0:T(1024)}, f32[1536]{0:T(1024)S(1)}, u32[]{:S(2)}) copy-start(f32[1536]{0:T(1024)S(1)} %convert_element_type.123) | copy-start | bytes 18436
  58.3 255.9 %copy-start.44 = (f32[128]{0:T(128)}, f32[128]{0:T(128)S(1)}, u32[]{:S(2)}) copy-start(f32[128]{0:T(128)S(1)} %get-tuple-element.676) | copy-start | bytes 1540
  133.3 184.5 %copy-start.22 = (f32[128,128]{0,1:T(8,128)}, f32[128,128]{0,1:T(8,128)S(1)}, u32[]{:S(2)}) copy-start(f32[128,128]{0,1:T(8,128)S(1)} %get-tuple-element.674) | copy-start | bytes 196612
  133.3 184.5 %copy-start.24 = (f32[128,128]{0,1:T(8,128)}, f32[128,128]{0,1:T(8,128)S(1)}, u32[]{:S(2)}) copy-start(f32[128,128]{0,1:T(8,128)S(1)} %get-tuple-element.673) | copy-start | bytes 196612
  666.8 180.0 %copy-start.17 = (bf16[128,1536]{1,0:T(8,128)(2,1)S(1)}, bf16[128,1536]{1,0:T(8,128)(2,1)}, u32[]{:S(2)}) copy-start(bf16[128,1536]{1,0:T(8,128)(2,1)} %param.39) | copy-start | bytes 1179652
  681.0 332.8 %all-gather.25.cloned.1.call-start = ((), (), s32[]{:S(2)}) async-start(), calls=%async_computation.15 | async-start | bytes 28385280 | tf_op jit(solution)/shard_map/all_gather | solution.py:213
  681.8 499.2 %all-gather.27.cloned.1.call-start = ((), (), s32[]{:S(2)}) async-start(), calls=%async_computation.16 | async-start | bytes 28385280 | tf_op jit(solution)/shard_map/all_gather | solution.py:214
  682.5 563.2 %all-gather.29.cloned.1.call-start = ((), (), s32[]{:S(2)}) async-start(), calls=%async_computation.17 | async-start | bytes 4866048 | tf_op jit(solution)/shard_map/all_gather | solution.py:206
  683.3 662.7 %reduce-scatter.12.cloned.1.call-start = ((), (), s32[]{:S(2)}) async-start(), calls=%async_computation.19 | async-start | bytes 1179648 | tf_op jit(solution)/shard_map/reduce_scatter | solution.py:362
  1283.5 129.3 %reduce-scatter.14.cloned.1.call-start = ((), (), s32[]{:S(2)}) async-start(), calls=%async_computation.20 | async-start | bytes 1179648 | tf_op jit(solution)/shard_map/reduce_scatter | solution.py:363
  1284.6 365.8 %all-gather.31.cloned.1.call-start = ((), (), s32[]{:S(2)}) async-start(), calls=%async_computation.18 | async-start | bytes 4866048 | tf_op jit(solution)/shard_map/all_gather | solution.py:200
  1285.2 413.3 %reduce-scatter.18.cloned.1.call-start = ((), (), s32[]{:S(2)}) async-start(), calls=%async_computation.22 | async-start | bytes 1622016 | tf_op jit(solution)/shard_map/reduce_scatter | solution.py:398
  1350.1 348.3 %reduce-scatter.20.cloned.1.call-start = ((), (), s32[]{:S(2)}) async-start(), calls=%async_computation.23 | async-start | bytes 1622016 | tf_op jit(solution)/shard_map/reduce_scatter | solution.py:399
  1415.4 408.4 %reduce-scatter.16.cloned.1.call-start = ((), (), s32[]{:S(2)}) async-start(), calls=%async_computation.21 | async-start | bytes 9732096 | tf_op jit(solution)/shard_map/reduce_scatter | solution.py:397
  1421.4 544.7 %reduce-scatter.22.cloned.1.call-start = ((), (), s32[]{:S(2)}) async-start(), calls=%async_computation.24 | async-start | bytes 9732096 | tf_op jit(solution)/shard_map/reduce_scatter | solution.py:400
  1427.6 1006.6 %reduce-scatter.28.cloned.1.call-start = ((), (), s32[]{:S(2)}) async-start(), calls=%async_computation.27 | async-start | bytes 56770560
  1451.8 1451.6 %reduce-scatter.24.cloned.1.call-start = ((), (), s32[]{:S(2)}) async-start(), calls=%async_computation.25 | async-start | bytes 56770560 | tf_op jit(solution)/shard_map/reduce_scatter | solution.py:401
  1476.4 1895.5 %reduce-scatter.26.cloned.1.call-start = ((), (), s32[]{:S(2)}) async-start(), calls=%async_computation.26 | async-start | bytes 56770560 | tf_op jit(solution)/shard_map/reduce_scatter | solution.py:402
  (54 other events, 1319.3 us)
Sparse Core Ops, SparseCore 0:
  10.9 70.2 all-gather.12
  84.2 66.2 all-gather.14
  153.4 178.7 all-gather.16
  335.0 164.8 all-gather.18
  502.6 164.1 all-gather.20
  681.2 165.6 all-gather.22
  849.7 164.0 all-gather.24
  1016.8 164.1 all-gather.26
  1183.9 61.8 all-gather.28
  1283.6 62.2 reduce-scatter.11
  1350.3 62.4 reduce-scatter.13
  1415.6 62.6 all-gather.30
  1484.1 96.5 reduce-scatter.17
  1586.4 96.4 reduce-scatter.19
  1689.2 134.5 reduce-scatter.15
  1831.2 134.8 reduce-scatter.21
  1972.9 461.1 reduce-scatter.27
  2442.2 461.2 reduce-scatter.23
  2910.5 461.3 reduce-scatter.25
where the time goes:
time: 3390 us; the launch traced here: 3380 us
  waiting for transfers between devices  2560 us (76%)
  blocking collectives  520 us (15%)
  matrix products  226 us (7%)
  local copies, waits for them, and re-layouts  34.5 us (1%)
    unnamed x20, waiting for transfers between devices  474 us
    reduce_scatter x1, waiting for transfers between devices, local(): lax.psum_scatter(gate_grad, ('batch', 'ctx'), scatter_dimension=0, tiled=...  469 us
    reduce_scatter x1, waiting for transfers between devices, local(): lax.psum_scatter(up_grad, ('batch', 'ctx'), scatter_dimension=0, tiled=True)  468 us
    all_gather x2, waiting for transfers between devices, gather_mlp(): lax.all_gather(w_up, ('batch', 'ctx'), axis=0, tiled=True)  291 us
    all_gather x2, waiting for transfers between devices, gather_mlp(): lax.all_gather(w_down, ('batch', 'ctx'), axis=0, tiled=True)  272 us
    all_gather x2, blocking collectives, gather_attention(): lax.all_gather(w_value, ('batch', 'ctx'), axis=0, tiled=True)  149 us
    all_gather x2, blocking collectives, gather_attention(): lax.all_gather(w_key, ('batch', 'ctx'), axis=0, tiled=True)  148 us
    all_gather x2, waiting for transfers between devices, gather_mlp(): lax.all_gather(w_gate, ('batch', 'ctx'), axis=0, tiled=True)  148 us
  transfers between devices with their start and end apart: 19, of which 13 were waited for; matrix products, arithmetic and copies ran while one was open for 7% of the time, Pallas kernels for 0%

commit v1 on v0

v1 whole, which is shorter than its diff:
```python
import math

import jax
import jax.numpy as jnp
from jax import lax
from jax.sharding import PartitionSpec as P

HEADS = 12
KV_HEADS = 2
GROUPS = HEADS // KV_HEADS
HEAD_DIM = 128
KVW = KV_HEADS * HEAD_DIM
INV_ROOT = HEAD_DIM ** (-0.5)
EPSILON = 1e-06
ROPE_BASE = 10000.0
MASKED = -1e30
ALL = ("batch", "ctx")
F32 = jnp.float32
BF16 = jnp.bfloat16


def rope_tables(positions):
    half_dim = HEAD_DIM // 2
    inverse_freq = jnp.exp(
        jnp.arange(half_dim, dtype=F32) * (-2.0 * math.log(ROPE_BASE) / HEAD_DIM)
    )
    angles = positions.astype(F32)[:, None] * inverse_freq[None, :]
    angles = jnp.concatenate([angles, angles], axis=1)
    return (jnp.cos(angles), jnp.sin(angles))


def rotate(values, cosine, sine_table):
    half_dim = values.shape[-1] // 2
    turned = jnp.concatenate([-values[..., half_dim:], values[..., :half_dim]], axis=-1)
    return values * cosine[:, None, :] + turned * sine_table[:, None, :]


def rotate_back(grad_rows, cosine, sine_table):
    half_dim = grad_rows.shape[-1] // 2
    scaled = grad_rows * sine_table[:, None, :]
    turned = jnp.concatenate([scaled[..., half_dim:], -scaled[..., :half_dim]], axis=-1)
    return grad_rows * cosine[:, None, :] + turned


def norm_rows(values, gain_vector):
    factor = lax.rsqrt(jnp.mean(values * values, axis=-1, keepdims=True) + EPSILON)
    return (values * factor * gain_vector, factor)


def norm_back(values, factor, gain_vector, grad_rows):
    scaled = grad_rows * gain_vector
    gain_grad = jnp.sum(grad_rows * values * factor, axis=0)
    value_grad = factor * scaled - values * (factor * factor * factor) * jnp.mean(
        scaled * values, axis=-1, keepdims=True
    )
    return (value_grad, gain_grad)


def dot(lhs, rhs):
    return jnp.dot(lhs, rhs, preferred_element_type=F32)


def contract_rows(lhs, rhs):
    return lax.dot_general(lhs, rhs, (((0,), (0,)), ((), ())), preferred_element_type=F32)


def times_transposed(lhs, rhs):
    return lax.dot_general(lhs, rhs, (((1,), (1,)), ((), ())), preferred_element_type=F32)


def lanes(width):
    return -(-width // 128) * 128


def pack_columns(weight, n_batch, n_ctx):
    rows, width = weight.shape
    piece = width // (n_batch * n_ctx)
    own = n_batch * piece
    packed = weight.reshape(rows, n_batch, n_ctx, piece).transpose(2, 0, 1, 3)
    packed = packed.reshape(n_ctx, rows, own)
    return jnp.pad(packed, ((0, 0), (0, 0), (0, lanes(own) - own)))


def unpack_columns(packed, n_batch, width):
    n_ctx, rows, _ = packed.shape
    piece = width // (n_batch * n_ctx)
    packed = packed[:, :, : n_batch * piece].reshape(n_ctx, rows, n_batch, piece)
    return packed.transpose(1, 2, 0, 3).reshape(rows, width)


def heads_of(rows):
    count = rows.shape[0]
    shaped = rows.reshape(count, KV_HEADS, GROUPS, HEAD_DIM).transpose(1, 2, 0, 3)
    return shaped.reshape(KV_HEADS, GROUPS * count, HEAD_DIM)


def rows_of(heads):
    count = heads.shape[1] // GROUPS
    shaped = heads.reshape(KV_HEADS, GROUPS, count, HEAD_DIM).transpose(2, 0, 1, 3)
    return shaped.reshape(count, HEADS * HEAD_DIM)


def kv_heads_of(rows):
    return rows.reshape(rows.shape[0], KV_HEADS, HEAD_DIM).transpose(1, 0, 2)


def own_slice(vector):
    width = vector.shape[0] // lax.axis_size(ALL)
    return lax.dynamic_slice_in_dim(vector, lax.axis_index(ALL) * width, width)


def local(
    hidden_in,
    positions,
    doc_ids,
    attn_gain,
    q_weight,
    q_bias,
    k_weight,
    k_bias,
    v_weight,
    v_bias,
    o_weight,
    mlp_gain,
    gate_weight,
    up_weight,
    down_weight,
    out_grad,
):
    n_batch, n_ctx = lax.axis_size("batch"), lax.axis_size("ctx")
    n_all = n_batch * n_ctx
    count, width = hidden_in.shape
    hidden_ff = gate_weight.shape[1]

    vectors = lax.all_gather(
        jnp.concatenate([attn_gain, mlp_gain, q_bias, k_bias, v_bias]), ALL, axis=0
    ).astype(F32)
    edges, at = [], 0
    for part in (attn_gain, mlp_gain, q_bias, k_bias, v_bias):
        edges.append(vectors[:, at : at + part.shape[0]].reshape(-1))
        at += part.shape[0]
    gain_one, gain_two, b_query, b_key, b_value = edges
    attn_all = lax.all_gather(
        jnp.concatenate([q_weight, k_weight, v_weight, o_weight], axis=1), ALL, axis=0, tiled=True
    )
    qkv_width = width + 2 * KVW
    w_qkv, w_out = attn_all[:, :qkv_width], attn_all[:, qkv_width:]
    b_qkv = jnp.concatenate([b_query, b_key, b_value])
    packed = jnp.concatenate(
        [pack_columns(gate_weight, n_batch, n_ctx), pack_columns(up_weight, n_batch, n_ctx)], axis=2
    )
    half = packed.shape[2] // 2
    packed = lax.all_to_all(packed, "ctx", split_axis=0, concat_axis=0)
    w_gate_up = lax.all_gather(packed.reshape(-1, 2 * half), "batch", axis=0, tiled=True)
    w_down = lax.all_gather(down_weight, "batch", axis=0, tiled=True)
    own_ff = w_down.shape[0]
    w_down = jnp.pad(w_down, ((0, half - own_ff), (0, 0)))
    out_grad_all = lax.all_gather(out_grad, "ctx", axis=0, tiled=True)

    cosine, sine_table = rope_tables(positions)
    hidden_wide = hidden_in.astype(F32)
    normed_wide, factor_one = norm_rows(hidden_wide, gain_one)
    normed_one = normed_wide.astype(BF16)
    lin = dot(normed_one, w_qkv) + b_qkv
    turned = rotate(
        lin[:, : width + KVW].reshape(count, HEADS + KV_HEADS, HEAD_DIM), cosine, sine_table
    ).astype(BF16).reshape(count, width + KVW)
    query_heads = heads_of(turned[:, :width])
    key_value = jnp.concatenate([turned[:, width:], lin[:, width + KVW :].astype(BF16)], axis=1)
    key_value = lax.all_gather(key_value, "ctx", axis=0, tiled=True)
    places = lax.all_gather(jnp.stack([positions, doc_ids]), "ctx", axis=1, tiled=True)
    key_heads, value_heads = kv_heads_of(key_value[:, :KVW]), kv_heads_of(key_value[:, KVW:])
    allowed = (places[0][None, :] <= positions[:, None]) & (places[1][None, :] == doc_ids[:, None])
    allowed = jnp.tile(allowed, (GROUPS, 1))
    scores = jnp.einsum("jqd,jkd->jqk", query_heads, key_heads, preferred_element_type=F32)
    scores = jnp.where(allowed[None], scores * INV_ROOT, MASKED)
    probs = jax.nn.softmax(scores, axis=-1)
    attn_probs = probs.astype(BF16)
    attn_out = rows_of(
        jnp.einsum("jqk,jkd->jqd", attn_probs, value_heads, preferred_element_type=F32)
    ).astype(BF16)
    residual = hidden_wide + dot(attn_out, w_out)

    normed_mid, factor_two = norm_rows(residual, gain_two)
    normed_two = lax.all_gather(normed_mid.astype(BF16), "ctx", axis=0, tiled=True)
    gate_up = dot(normed_two, w_gate_up)
    gate_lin, up_lin = gate_up[:, :half], gate_up[:, half:]
    sigmoid_gate = jax.nn.sigmoid(gate_lin)
    mixed_rows = (gate_lin * sigmoid_gate * up_lin).astype(BF16)
    d_mixed = times_transposed(out_grad_all, w_down)
    d_gate = d_mixed * up_lin * sigmoid_gate * (1.0 + gate_lin * (1.0 - sigmoid_gate))
    d_up = d_mixed * (gate_lin * sigmoid_gate)
    d_gate_up = jnp.concatenate([d_gate.astype(BF16), d_up.astype(BF16)], axis=1)
    d_normed_two = lax.psum_scatter(
        times_transposed(d_gate_up, w_gate_up).astype(BF16), "ctx", scatter_dimension=0, tiled=True
    ).astype(F32)
    ff_out = lax.psum_scatter(
        dot(mixed_rows, w_down).astype(BF16), "ctx", scatter_dimension=0, tiled=True
    )
    hidden_out = (residual + ff_out.astype(F32)).astype(BF16)
    down_grad = contract_rows(mixed_rows, out_grad_all)[:own_ff].astype(BF16)
    down_grad = lax.psum_scatter(down_grad, "batch", scatter_dimension=0, tiled=True)
    gate_up_grad = contract_rows(normed_two, d_gate_up).astype(BF16)
    gate_up_grad = lax.psum_scatter(gate_up_grad, "batch", scatter_dimension=0, tiled=True)
    gate_up_grad = lax.all_to_all(
        gate_up_grad.reshape(n_ctx, -1, 2 * half), "ctx", split_axis=0, concat_axis=0
    ).astype(F32)
    gate_grad = unpack_columns(gate_up_grad[:, :, :half], n_batch, hidden_ff)
    up_grad = unpack_columns(gate_up_grad[:, :, half:], n_batch, hidden_ff)

    d_residual_norm, gain_two_grad = norm_back(residual, factor_two, gain_two, d_normed_two)
    d_residual = out_grad.astype(F32) + d_residual_norm
    d_branch = d_residual.astype(BF16)
    out_proj_grad = contract_rows(attn_out, d_branch)
    grad_heads = heads_of(times_transposed(d_branch, w_out).astype(BF16))
    d_probs = jnp.einsum("jqd,jkd->jqk", grad_heads, value_heads, preferred_element_type=F32)
    row_delta = jnp.sum(probs * d_probs, axis=-1, keepdims=True)
    d_scores = (probs * (d_probs - row_delta)).astype(BF16)
    d_queries = rows_of(
        jnp.einsum("jqk,jkd->jqd", d_scores, key_heads, preferred_element_type=F32) * INV_ROOT
    )
    d_keys = jnp.einsum("jqk,jqd->kjd", d_scores, query_heads, preferred_element_type=F32) * INV_ROOT
    d_values = jnp.einsum("jqk,jqd->kjd", attn_probs, grad_heads, preferred_element_type=F32)
    d_key_value = jnp.concatenate([d_keys.reshape(-1, KVW), d_values.reshape(-1, KVW)], axis=1)
    d_key_value = lax.psum_scatter(
        d_key_value.astype(BF16), "ctx", scatter_dimension=0, tiled=True
    ).astype(F32)
    d_turned = jnp.concatenate([d_queries, d_key_value[:, :KVW]], axis=1)
    d_turned = rotate_back(
        d_turned.reshape(count, HEADS + KV_HEADS, HEAD_DIM), cosine, sine_table
    ).reshape(count, width + KVW)
    d_lin = jnp.concatenate([d_turned, d_key_value[:, KVW:]], axis=1).astype(BF16)
    qkv_grad = contract_rows(normed_one, d_lin)
    bias_grad = jnp.sum(d_lin.astype(F32), axis=0)
    d_normed_one = times_transposed(d_lin, w_qkv)
    d_hidden_norm, gain_one_grad = norm_back(hidden_wide, factor_one, gain_one, d_normed_one)
    hidden_grad = d_residual + d_hidden_norm

    attn_grads = jnp.concatenate([qkv_grad.astype(BF16), out_proj_grad.astype(BF16)], axis=1)
    attn_grads = lax.psum_scatter(attn_grads, ALL, scatter_dimension=0, tiled=True).astype(F32)
    sums = lax.psum(jnp.concatenate([gain_one_grad, bias_grad, gain_two_grad]), ALL)
    at_key, at_value, at_out = width, width + KVW, width + 2 * KVW
    return (
        hidden_out,
        hidden_grad,
        own_slice(sums[:width]),
        attn_grads[:, :at_key],
        own_slice(sums[width : 2 * width]),
        attn_grads[:, at_key:at_value],
        own_slice(sums[2 * width : 2 * width + KVW]),
        attn_grads[:, at_value:at_out],
        own_slice(sums[2 * width + KVW : 2 * width + 2 * KVW]),
        attn_grads[:, at_out:],
        own_slice(sums[2 * width + 2 * KVW :]),
        gate_grad,
        up_grad,
        lax.convert_element_type(down_grad, F32),
    )


def solution(mesh):
    matrix, vector = P(ALL, None), P(ALL)
    placed = (
        (matrix, vector, vector, vector, matrix, vector, matrix, vector)
        + (matrix, vector, matrix, vector, matrix, matrix, matrix, matrix)
    )
    results = (matrix, matrix) + (vector, matrix) * 4 + (vector, matrix, matrix, matrix)
    return jax.shard_map(local, mesh=mesh, in_specs=placed, out_specs=results, check_vma=False)
```

time: 3390 us -> 928 us (0.27)
  waiting for transfers between devices: 2560 us -> 549 us
  blocking collectives: 520 us -> 139 us
  matrix products: 226 us -> 108 us
    reduce_scatter x8 -> x5, waiting for transfers between devices: 1330 us -> 306 us  [the longest x1 76.5 us: local(): lax.psum_scatter(attn_grads, ALL, scatter_dimension=0, tiled=True)]
    all_gather x10 -> x6, waiting for transfers between devices: 758 us -> 209 us  [the longest x1 63.1 us: local(): lax.all_gather(normed_mid.astype(BF16), 'ctx', axis=0, tiled=True)]
    unnamed x20 -> x13, waiting for transfers between devices: 474 us -> 33.7 us
    all_gather x8 -> x1, blocking collectives: 399 us -> 19.2 us  [local(): lax.all_gather(jnp.stack([positions, doc_ids]), 'ctx', axis=1, tiled=True)]
    dot_general x39 -> x17, matrix products: 226 us -> 103 us  [the longest x4 34.3 us: times_transposed(): lax.dot_general(lhs, rhs, (((1,), (1,)), ((), ())), preferred_element_typ...]
    unnamed x2 -> x1, blocking collectives: 82.4 us -> 79.9 us
  transfers between devices with their start and end apart: 19 -> 14, of which waited for: 13 -> 12; matrix products, arithmetic and copies ran while one was open for 7% -> 16% of each run, Pallas kernels for 0% -> 0%
where the time goes in v1:
time: 928 us; the launch traced here: 919 us
  waiting for transfers between devices  549 us (59%)
  blocking collectives  139 us (15%)
  matrix products  108 us (12%)
  local copies, waits for them, and re-layouts  61.1 us (7%)
  other arithmetic  32.6 us (4%)
  between operations  15.3 us (2%)
  starting transfers between devices  13.7 us (1%)
    unnamed x1, blocking collectives  79.9 us
    reduce_scatter x1, waiting for transfers between devices, local(): lax.psum_scatter(attn_grads, ALL, scatter_dimension=0, tiled=True)  76.5 us
    reduce_scatter x1, waiting for transfers between devices, local(): lax.psum_scatter(dot(mixed_rows, w_down).astype(BF16), 'ctx', scatter_dim...  75.8 us
    reduce_scatter x1, waiting for transfers between devices, local(): lax.psum_scatter(times_transposed(d_gate_up, w_gate_up).astype(BF16), 'ct...  64.3 us
    all_gather x1, waiting for transfers between devices, local(): lax.all_gather(normed_mid.astype(BF16), 'ctx', axis=0, tiled=True)  63.1 us
    all_gather x1, waiting for transfers between devices, local(): out_grad_all = lax.all_gather(out_grad, 'ctx', axis=0, tiled=True)  62.5 us
    reduce_scatter x1, waiting for transfers between devices, local(): lax.psum_scatter(gate_up_grad, 'batch', scatter_dimension=0, tiled=True)  52.5 us
    psum x1, blocking collectives, local(): lax.psum(jnp.concatenate([gain_one_grad, bias_grad, gain_two_grad]), ALL)  39.8 us
  transfers between devices with their start and end apart: 14, of which 12 were waited for; matrix products, arithmetic and copies ran while one was open for 16% of the time, Pallas kernels for 0%

profile of v1, /device:TPU:0, one launch (start us, length us, event | category | flops | bytes accessed | tf_op | source)
XLA Modules:
  0.0 918.7 jit_solution(5282277173943277176)
XLA Ops:
  21.2 7.3 all-to-all-start
  28.9 79.9 %all-reduce.3 = bf16[5120]{0:T(1024)(128)(2,1)S(1)} all-reduce(bf16[5120]{0:T(1024)(128)(2,1)S(1)} %dynamic-update-slice), channel_id=2, replica_groups=mesh['batch'=4,'ctx'=8] {'batch','ctx'}, use_global_device_ids=true, to_apply=%add.3 | all-reduce | flops 5120 | bytes 20480
  112.9 16.1 %all-gather.8.cloned.1.call-done = bf16[1536,3584]{1,0:T(8,128)(2,1)} async-done(((bf16[48,3584]{1,0:T(8,128)(2,1)}), bf16[1536,3584]{1,0:T(8,128)(2,1)}) %all-gather.8.cloned.1.call-update) | async-done | bytes 11010064 | tf_op jit(solution)/shard_map/all_gather | solution.py:143
  145.1 19.2 %all_gather.27 = s32[2,1024]{1,0:T(2,128)S(1)} all-gather(s32[2,128]{1,0:T(2,128)S(1)} %pad_add_fusion), channel_id=1, replica_groups=mesh['batch'=4,'ctx'=8] {'ctx'}, dimensions={1}, use_global_device_ids=true | all-gather | bytes 9216 | tf_op jit(solution)/shard_map/all_gather | solution.py:171
  165.0 16.5 %all-gather.10.cloned.1.call-done = bf16[1024,512]{1,0:T(8,128)(2,1)} async-done(((bf16[128,512]{1,0:T(8,128)(2,1)}), bf16[1024,512]{1,0:T(8,128)(2,1)}) %all-gather.10.cloned.1.call-update) | async-done | bytes 1048592 | tf_op jit(solution)/shard_map/all_gather | solution.py:170
  198.7 34.0 %all-gather.14.cloned.1.call-done = bf16[1536,2304]{1,0:T(8,128)(2,1)} async-done(((bf16[384,2304]{1,0:T(8,128)(2,1)}), bf16[1536,2304]{1,0:T(8,128)(2,1)}) %all-gather.14.cloned.1.call-update) | async-done | bytes 7077904 | tf_op jit(solution)/shard_map/all_gather | solution.py:154
  232.7 63.1 %all-gather.12.cloned.1.call-done = bf16[1024,1536]{1,0:T(8,128)(2,1)} async-done(((bf16[128,1536]{1,0:T(8,128)(2,1)}), bf16[1024,1536]{1,0:T(8,128)(2,1)}) %all-gather.12.cloned.1.call-update) | async-done | bytes 3145744 | tf_op jit(solution)/shard_map/all_gather | solution.py:185
  295.8 13.3 %fusion.97 = f32[1024,2304]{1,0:T(8,128)} fusion(bf16[1024,1536]{1,0:T(8,128)(2,1)} %all-gather.12.cloned.1.call-done, bf16[1536,2304]{1,0:T(8,128)(2,1)} %all-gather.14.cloned.1.call-done), kind=kOutput, calls=%fused_computation.148 | convolution fusion | flops 7247757312 | bytes 19660800 | tf_op jit(solution)/shard_map/dot_general | solution.py:60
  309.1 17.0 %all-gather.16.cloned.1.call-done = bf16[1120,1536]{1,0:T(8,128)(2,1)} async-done(((bf16[280,1536]{1,0:T(8,128)(2,1)}), bf16[1120,1536]{1,0:T(8,128)(2,1)}) %all-gather.16.cloned.1.call-update) | async-done | bytes 3440656 | tf_op jit(solution)/shard_map/all_gather | solution.py:155
  326.1 62.5 %all-gather.18.cloned.1.call-done = bf16[1024,1536]{1,0:T(8,128)(2,1)} async-done(((bf16[128,1536]{1,0:T(8,128)(2,1)}), bf16[1024,1536]{1,0:T(8,128)(2,1)}) %all-gather.18.cloned.1.call-update) | async-done | bytes 3145744 | tf_op jit(solution)/shard_map/all_gather | solution.py:158
  388.6 12.5 %fusion.8 = (bf16[1024,1152]{1,0:T(8,128)(2,1)S(1)}, bf16[1024,1152]{1,0:T(8,128)(2,1)S(1)}, bf16[1024,1152]{1,0:T(8,128)(2,1)}) fusion(f32[1024,2304]{1,0:T(8,128)} %fusion.97, bf16[1024,1536]{1,0:T(8,128)(2,1)} %all-gather.18.cloned.1.call-done, bf16[1120,1536]{1,0:T(8,128)(2,1)} %all-gather.16.cloned.1.call-done), kind=kOutput, calls=%fused_computation.20 | convolution fusion | flops 3641573376 | bytes 23101440 | tf_op jit(solution)/shard_map/dot_general | solution.py:68
  403.3 10.9 %convolution_convert_fusion.3 = bf16[1024,1536]{1,0:T(8,128)(2,1)} fusion(bf16[1536,2304]{1,0:T(8,128)(2,1)} %all-gather.14.cloned.1.call-done, bf16[1024,1152]{1,0:T(8,128)(2,1)S(1)} %get-tuple-element.19, bf16[1024,1152]{1,0:T(8,128)(2,1)S(1)} %get-tuple-element.18), kind=kOutput, calls=%fused_computation.29 | convolution fusion | flops 7258767360 | bytes 14942208 | tf_op jit(solution)/shard_map/dot_general | solution.py:68
  414.3 8.6 convolution_convert_fusion.4
  423.1 64.3 %reduce-scatter.11.cloned.1.call-done = bf16[128,1536]{1,0:T(8,128)(2,1)} async-done(((bf16[1024,1536]{1,0:T(8,128)(2,1)}), bf16[128,1536]{1,0:T(8,128)(2,1)}) %reduce-scatter.11.cloned.1.call-update) | async-done | bytes 393232 | tf_op jit(solution)/shard_map/reduce_scatter | solution.py:194
  488.6 75.8 %reduce-scatter.9.cloned.1.call-done = bf16[128,1536]{1,0:T(8,128)(2,1)} async-done(((bf16[1024,1536]{1,0:T(8,128)(2,1)}), bf16[128,1536]{1,0:T(8,128)(2,1)}) %reduce-scatter.9.cloned.1.call-update) | async-done | bytes 393232 | tf_op jit(solution)/shard_map/reduce_scatter | solution.py:197
  587.1 12.4 %convolution_convert_fusion = bf16[1536,2304]{1,0:T(8,128)(2,1)} fusion(bf16[1024,1536]{1,0:T(8,128)(2,1)} %all-gather.12.cloned.1.call-done, bf16[1024,1152]{1,0:T(8,128)(2,1)} %copy-done.26, bf16[1024,1152]{1,0:T(8,128)(2,1)} %copy-done.25), kind=kOutput, calls=%fused_computation.1 | convolution fusion | flops 7260733440 | bytes 14942208 | tf_op jit(solution)/shard_map/dot_general | solution.py:64
  599.9 6.5 fusion.98
  617.5 32.5 %reduce-scatter.19.cloned.1.call-done = bf16[128,512]{1,0:T(8,128)(2,1)} async-done(((bf16[1024,512]{1,0:T(8,128)(2,1)}), bf16[128,512]{1,0:T(8,128)(2,1)}) %reduce-scatter.19.cloned.1.call-update) | async-done | bytes 131088
  656.7 5.9 pad_maximum_fusion
  662.6 52.5 %reduce-scatter.15.cloned.1.call-done = bf16[384,2304]{1,0:T(8,128)(2,1)} async-done(((bf16[1536,2304]{1,0:T(8,128)(2,1)}), bf16[384,2304]{1,0:T(8,128)(2,1)}) %reduce-scatter.15.cloned.1.call-update) | async-done | bytes 1769488 | tf_op jit(solution)/shard_map/reduce_scatter | solution.py:204
  720.7 36.9 %reduce-scatter.17.cloned.1.call-done = bf16[280,1536]{1,0:T(8,128)(2,1)} async-done(((bf16[1120,1536]{1,0:T(8,128)(2,1)}), bf16[280,1536]{1,0:T(8,128)(2,1)}) %reduce-scatter.17.cloned.1.call-update) | async-done | bytes 860176 | tf_op jit(solution)/shard_map/reduce_scatter | solution.py:202
  760.4 6.0 fusion.60
  766.4 39.8 %psum.7 = f32[5120]{0:T(1024)S(1)} all-reduce(f32[5120]{0:T(1024)S(1)} %pad_maximum_fusion.13), channel_id=1, replica_groups=mesh['batch'=4,'ctx'=8] {'batch','ctx'}, use_global_device_ids=true, to_apply=%region_13.14 | all-reduce | flops 5120 | bytes 40960 | tf_op jit(solution)/shard_map/psum | solution.py:241
  831.6 76.5 %reduce-scatter.13.cloned.1.call-done = bf16[48,3584]{1,0:T(8,128)(2,1)} async-done(((bf16[1536,3584]{1,0:T(8,128)(2,1)}), bf16[48,3584]{1,0:T(8,128)(2,1)}) %reduce-scatter.13.cloned.1.call-update) | async-done | bytes 344080 | tf_op jit(solution)/shard_map/reduce_scatter | solution.py:240
  (190 shorter events, 133.3 us)
Async XLA Ops:
  7.2 121.8 %all-gather.8.cloned.1.call-start = ((), (), s32[]{:S(2)}) async-start(), calls=%async_computation.8 | async-start | bytes 11354112 | tf_op jit(solution)/shard_map/all_gather | solution.py:143
  17.7 92.3 %copy-start.17 = (s32[128]{0:T(128)S(1)}, s32[128]{0:T(128)}, u32[]{:S(2)}) copy-start(s32[128]{0:T(128)} %param.17) | copy-start | bytes 1540
  18.5 93.8 %copy-start.3 = (bf16[128,1536]{1,0:T(8,128)(2,1)S(1)}, bf16[128,1536]{1,0:T(8,128)(2,1)}, u32[]{:S(2)}) copy-start(bf16[128,1536]{1,0:T(8,128)(2,1)} %param.16) | copy-start | bytes 1179652
  21.2 121.7 %all-to-all-start = ((bf16[8,48,2304]{2,1,0:T(8,128)(2,1)}), bf16[8,48,2304]{2,1,0:T(8,128)(2,1)S(1)}, u32[]{:S(2)}, u32[]{:S(2)}) async-start(bf16[8,48,2304]{2,1,0:T(8,128)(2,1)} %fusion.32), calls=%async_computation | async-start | bytes 3538944 | tf_op jit(solution)/shard_map/all_to_all | solution.py:153
  28.4 153.1 %all-gather.10.cloned.1.call-start = ((), (), s32[]{:S(2)}) async-start(), calls=%async_computation.9 | async-start | bytes 1179648 | tf_op jit(solution)/shard_map/all_gather | solution.py:170
  142.8 89.9 %all-gather.14.cloned.1.call-start = ((), (), s32[]{:S(2)}) async-start(), calls=%async_computation.11 | async-start | bytes 8847360 | tf_op jit(solution)/shard_map/all_gather | solution.py:154
  144.2 151.6 %all-gather.12.cloned.1.call-start = ((), (), s32[]{:S(2)}) async-start(), calls=%async_computation.10 | async-start | bytes 3538944 | tf_op jit(solution)/shard_map/all_gather | solution.py:185
  165.0 23.2 %copy-start.8 = (bf16[2,6,128,128]{3,2,1,0:T(8,128)(2,1)}, bf16[2,6,128,128]{3,2,1,0:T(8,128)(2,1)S(1)}, u32[]{:S(2)}) copy-start(bf16[2,6,128,128]{3,2,1,0:T(8,128)(2,1)S(1)} %copy.66) | copy-start | bytes 1179652
  188.2 390.5 %copy-start.14 = (f32[2,768]{1,0:T(2,128)}, f32[2,768]{1,0:T(2,128)S(1)}, u32[]{:S(2)}) copy-start(f32[2,768]{1,0:T(2,128)S(1)} %get-tuple-element.55) | copy-start | bytes 18436
  193.1 116.0 %copy-start.5 = (bf16[2,6,128,128]{2,3,1,0:T(8,128)(2,1)}, bf16[2,6,128,128]{2,3,1,0:T(8,128)(2,1)S(1)}, u32[]{:S(2)}) copy-start(bf16[2,6,128,128]{2,3,1,0:T(8,128)(2,1)S(1)} %copy.69) | copy-start | bytes 1179652
  197.5 128.6 %all-gather.16.cloned.1.call-start = ((), (), s32[]{:S(2)}) async-start(), calls=%async_computation.12 | async-start | bytes 4300800 | tf_op jit(solution)/shard_map/all_gather | solution.py:155
  198.1 190.6 %all-gather.18.cloned.1.call-start = ((), (), s32[]{:S(2)}) async-start(), calls=%async_computation.14 | async-start | bytes 3538944 | tf_op jit(solution)/shard_map/all_gather | solution.py:158
  198.7 288.7 %reduce-scatter.11.cloned.1.call-start = ((), (), s32[]{:S(2)}) async-start(), calls=%async_computation.15 | async-start | bytes 3538944 | tf_op jit(solution)/shard_map/reduce_scatter | solution.py:194
  414.2 150.2 %reduce-scatter.9.cloned.1.call-start = ((), (), s32[]{:S(2)}) async-start(), calls=%async_computation.13 | async-start | bytes 3538944 | tf_op jit(solution)/shard_map/reduce_scatter | solution.py:197
  414.3 150.1 %copy-start.7 = (bf16[128,1536]{1,0:T(8,128)(2,1)S(1)}, bf16[128,1536]{1,0:T(8,128)(2,1)}, u32[]{:S(2)}) copy-start(bf16[128,1536]{1,0:T(8,128)(2,1)} %param.31) | copy-start | bytes 1179652
  422.9 227.0 %reduce-scatter.19.cloned.1.call-start = ((), (), s32[]{:S(2)}) async-start(), calls=%async_computation.19 | async-start | bytes 1179648
  587.1 128.1 %reduce-scatter.15.cloned.1.call-start = ((), (), s32[]{:S(2)}) async-start(), calls=%async_computation.17 | async-start | bytes 8847360 | tf_op jit(solution)/shard_map/reduce_scatter | solution.py:204
  599.6 158.0 %reduce-scatter.17.cloned.1.call-start = ((), (), s32[]{:S(2)}) async-start(), calls=%async_computation.18 | async-start | bytes 4300800 | tf_op jit(solution)/shard_map/reduce_scatter | solution.py:202
  608.3 299.8 %reduce-scatter.13.cloned.1.call-start = ((), (), s32[]{:S(2)}) async-start(), calls=%async_computation.16 | async-start | bytes 11354112 | tf_op jit(solution)/shard_map/reduce_scatter | solution.py:240
  612.7 39.0 %copy-start.12 = (f32[128,128]{0,1:T(8,128)S(1)}, f32[128,128]{0,1:T(8,128)}, u32[]{:S(2)}) copy-start(f32[128,128]{0,1:T(8,128)} %get-tuple-element.41) | copy-start | bytes 196612
  662.6 97.8 %copy-start.16 = (f32[128]{0:T(128)S(1)}, f32[128]{0:T(128)}, u32[]{:S(2)}) copy-start(f32[128]{0:T(128)} %copy-done.15) | copy-start | bytes 1540
  715.2 96.3 %all-to-all-start.1 = ((bf16[8,48,2304]{2,1,0:T(8,128)(2,1)}), bf16[8,48,2304]{2,1,0:T(8,128)(2,1)S(1)}, u32[]{:S(2)}, u32[]{:S(2)}) async-start(bf16[8,48,2304]{2,1,0:T(8,128)(2,1)} %bitcast.144), calls=%async_computation.5 | async-start | bytes 3538944 | tf_op jit(solution)/shard_map/all_to_all | solution.py:205
  760.4 48.7 %copy-start.2 = (f32[128,1536]{1,0:T(8,128)S(1)}, f32[128,1536]{1,0:T(8,128)}, u32[]{:S(2)}) copy-start(f32[128,1536]{1,0:T(8,128)} %copy-done.1) | copy-start | bytes 2359300
  760.4 48.7 %copy-start.24 = (f32[128]{0:T(128)S(1)}, f32[128]{0:T(128)}, u32[]{:S(2)}) copy-start(f32[128]{0:T(128)} %get-tuple-element.51) | copy-start | bytes 1540
  (21 other events, 151.5 us)
Sparse Core Ops, SparseCore 0:
  11.5 117.4 all-gather.7
  142.9 38.5 all-gather.9
  183.1 49.5 all-gather.13
  235.4 60.4 all-gather.11
  297.3 28.8 all-gather.15
  328.2 60.4 all-gather.17
  414.4 72.9 reduce-scatter.10
  491.0 73.3 reduce-scatter.8
  587.2 62.6 reduce-scatter.18
  652.5 62.6 reduce-scatter.14
  717.7 39.8 reduce-scatter.16
  764.5 143.6 reduce-scatter.12

commit v2 on v1

--- a/solution.py
+++ b/solution.py
@@ -1,8 +1,11 @@
+import functools
 import math
 
 import jax
 import jax.numpy as jnp
 from jax import lax
+from jax.experimental import pallas as pl
+from jax.experimental.pallas import tpu as pltpu
 from jax.sharding import PartitionSpec as P
 
 HEADS = 12
@@ -17,6 +20,10 @@
 ALL = ("batch", "ctx")
 F32 = jnp.float32
 BF16 = jnp.bfloat16
+MESH = pl.DeviceIdType.MESH
+ANYWHERE = pl.BlockSpec(memory_space=pl.ANY)
+IN_VMEM = pl.BlockSpec(memory_space=pltpu.VMEM)
+DMA = pltpu.SemaphoreType.DMA
 
 
 def rope_tables(positions):
@@ -104,9 +111,360 @@
     return rows.reshape(rows.shape[0], KV_HEADS, HEAD_DIM).transpose(1, 0, 2)
 
 
-def own_slice(vector):
-    width = vector.shape[0] // lax.axis_size(ALL)
-    return lax.dynamic_slice_in_dim(vector, lax.axis_index(ALL) * width, width)
+def greet(devices):
+    barrier = pltpu.get_barrier_semaphore()
+    for device in devices:
+        pl.semaphore_signal(barrier, inc=1, device_id=device, device_id_type=MESH)
+    pl.semaphore_wait(barrier, len(devices))
+
+
+def remote(source, target, send, receive, device):
+    return pltpu.make_async_remote_copy(
+        src_ref=source,
+        dst_ref=target,
+        send_sem=send,
+        recv_sem=receive,
+        device_id=device,
+        device_id_type=MESH,
+    )
+
+
+def gather_kernel(line_len, own, out, own_sem, line_sems, pair_sems):
+    b, c = lax.axis_index("batch"), lax.axis_index("ctx")
+    line, pair = c // 2, c % 2
+    ahead = (b, 2 * lax.rem(line + 1, line_len) + pair)
+    behind = (b, 2 * lax.rem(line + line_len - 1, line_len) + pair)
+    across = (b, c ^ 1)
+    greet((ahead, behind, across))
+    keep = pltpu.make_async_copy(own, out.at[c], own_sem)
+    keep.start()
+    on_line, on_pair = [], []
+    for step in range(line_len):
+        at = 2 * lax.rem(line - step + line_len, line_len) + pair
+        block = own if step == 0 else out.at[at]
+        if step > 0:
+            on_line[step - 1].wait_recv()
+        if step < line_len - 1:
+            copy = remote(block, out.at[at], line_sems.at[0, step], line_sems.at[1, step], ahead)
+            copy.start()
+            on_line.append(copy)
+        copy = remote(block, out.at[at], pair_sems.at[0, step], pair_sems.at[1, step], across)
+        copy.start()
+        on_pair.append(copy)
+    for copy in on_pair:
+        copy.wait()
+    for copy in on_line:
+        copy.wait_send()
+    keep.wait()
+
+
+def gather_ctx(block, collective_id, name):
+    n_ctx = lax.axis_size("ctx")
+    line_len = n_ctx // 2
+    return pl.pallas_call(
+        functools.partial(gather_kernel, line_len),
+        out_shape=jax.ShapeDtypeStruct((n_ctx,) + block.shape, block.dtype),
+        in_specs=[ANYWHERE],
+        out_specs=ANYWHERE,
+        scratch_shapes=[DMA(()), DMA((2, line_len)), DMA((2, line_len))],
+        compiler_params=pltpu.CompilerParams(collective_id=collective_id, has_side_effects=True),
+        name=name,
+    )(block)
+
+
+def scatter_kernel(
+    line_len, parts, out, pair_in, line_in, line_out, pair_sems, line_sems
+):
+    b, c = lax.axis_index("batch"), lax.axis_index("ctx")
+    line, pair = c // 2, c % 2
+    ahead = (b, 2 * lax.rem(line + 1, line_len) + pair)
+    behind = (b, 2 * lax.rem(line + line_len - 1, line_len) + pair)
+    across = (b, c ^ 1)
+    greet((ahead, behind, across))
+    given, passed = [], []
+    for step in range(line_len):
+        to = lax.rem(line - 1 - step + line_len, line_len)
+        copy = remote(
+            parts.at[2 * to + 1 - pair],
+            pair_in.at[step],
+            pair_sems.at[0, step],
+            pair_sems.at[1, step],
+            across,
+        )
+        copy.start()
+        given.append(copy)
+    for step in range(line_len):
+        to = lax.rem(line - 1 - step + line_len, line_len)
+        given[step].wait_recv()
+        total = parts[2 * to + pair].astype(F32) + pair_in[step].astype(F32)
+        if step > 0:
+            passed[step - 1].wait_recv()
+            total = total + line_in[step - 1].astype(F32)
+        if step < line_len - 1:
+            line_out[step] = total.astype(line_out.dtype)
+            copy = remote(
+                line_out.at[step],
+                line_in.at[step],
+                line_sems.at[0, step],
+                line_sems.at[1, step],
+                ahead,
+            )
+            copy.start()
+            passed.append(copy)
+        else:
+            out[...] = total
+    for copy in given + passed:
+        copy.wait_send()
+
+
+def scatter_ctx(parts, collective_id, name):
+    n_ctx = lax.axis_size("ctx")
+    line_len = n_ctx // 2
+    block = (parts.shape[0] // n_ctx,) + parts.shape[1:]
+    return pl.pallas_call(
+        functools.partial(scatter_kernel, line_len),
+        out_shape=jax.ShapeDtypeStruct(block, F32),
+        in_specs=[IN_VMEM],
+        out_specs=IN_VMEM,
+        scratch_shapes=[
+            pltpu.VMEM((line_len,) + block, parts.dtype),
+            pltpu.VMEM((line_len - 1,) + block, parts.dtype),
+            pltpu.VMEM((line_len - 1,) + block, parts.dtype),
+            DMA((2, line_len)),
+            DMA((2, line_len)),
+        ],
+        compiler_params=pltpu.CompilerParams(
+            collective_id=collective_id, has_side_effects=True, vmem_limit_bytes=56 * 2**20
+        ),
+        name=name,
+    )(parts.reshape((n_ctx,) + block))
+
+
+def spread_kernel(
+    line_len, own, columns, out, columns_out, own_sem, line_sems, pair_sems, chip_sems, core_sems,
+    column_sems,
+):
+    b, c = lax.axis_index("batch"), lax.axis_index("ctx")
+    n_ctx = 2 * line_len
+    line, pair = c // 2, c % 2
+    ahead = (b, 2 * lax.rem(line + 1, line_len) + pair)
+    across, chip, core = (b, c ^ 1), (b ^ 2, c), (b ^ 1, c)
+    others = [(b, lax.rem(c + k, n_ctx)) for k in range(1, n_ctx)]
+    greet([chip, core] + others)
+    keep = [
+        pltpu.make_async_copy(own, out.at[b, c], own_sem.at[0]),
+        pltpu.make_async_copy(columns.at[c], columns_out.at[c], own_sem.at[1]),
+    ]
+    for copy in keep:
+        copy.start()
+
+    def place(step, side):
+        return 2 * lax.rem(line - step + line_len, line_len) + side
+
+    def hand(block, to_b, to_c, sems, index, device):
+        copy = remote(block, out.at[to_b, to_c], sems.at[0, index], sems.at[1, index], device)
+        copy.start()
+        return copy
+
+    on_line, on_pair, on_chip, on_core, on_columns = [], [], [], [], []
+    for step in range(line_len):
+        at = place(step, pair)
+        block = own if step == 0 else out.at[b, at]
+        if step > 0:
+            on_line[step - 1].wait_recv()
+        if step < line_len - 1:
+            on_line.append(hand(block, b, at, line_sems, step, ahead))
+        on_pair.append(hand(block, b, at, pair_sems, step, across))
+        on_chip.append(hand(block, b, at, chip_sems, step, chip))
+        on_core.append(hand(block, b, at, core_sems, step, core))
+    for k, device in enumerate(others):
+        copy = remote(
+            columns.at[device[1]],
+            columns_out.at[c],
+            column_sems.at[0, k],
+            column_sems.at[1, k],
+            device,
+        )
+        copy.start()
+        on_columns.append(copy)
+    for step in range(line_len):
+        at = place(step, 1 - pair)
+        on_pair[step].wait_recv()
+        on_chip.append(hand(out.at[b, at], b, at, chip_sems, line_len + step, chip))
+        on_core.append(hand(out.at[b, at], b, at, core_sems, line_len + step, core))
+    for index in range(n_ctx):
+        at = place(index % line_len, pair if index < line_len else 1 - pair)
+        on_chip[index].wait_recv()
+        on_core.append(hand(out.at[b ^ 2, at], b ^ 2, at, core_sems, n_ctx + index, core))
+    for copy in on_core + on_columns:
+        copy.wait()
+    for copy in on_line + on_pair + on_chip:
+        copy.wait_send()
+    for copy in keep:
+        copy.wait()
+
+
+def spread(own, columns, collective_id, name):
+    n_batch, n_ctx = lax.axis_size("batch"), lax.axis_size("ctx")
+    line_len = n_ctx // 2
+    return pl.pallas_call(
+        functools.partial(spread_kernel, line_len),
+        out_shape=(
+            jax.ShapeDtypeStruct((n_batch, n_ctx) + own.shape, own.dtype),
+            jax.ShapeDtypeStruct(columns.shape, columns.dtype),
+        ),
+        in_specs=[ANYWHERE, ANYWHERE],
+        out_specs=(ANYWHERE, ANYWHERE),
+        scratch_shapes=[
+            DMA((2,)),
+            DMA((2, line_len)),
+            DMA((2, line_len)),
+            DMA((2, n_ctx)),
+            DMA((2, 2 * n_ctx)),
+            DMA((2, n_ctx)),
+        ],
+        compiler_params=pltpu.CompilerParams(collective_id=collective_id, has_side_effects=True),
+        name=name,
+    )(own, columns)
+
+
+def collect_kernel(
+    line_len, grads, columns, out, columns_out, core_in, chip_in, pair_in, line_in, chip_out,
+    pair_out, line_out, own_sem, core_sems, chip_sems, pair_sems, line_sems, column_sems,
+):
+    b, c = lax.axis_index("batch"), lax.axis_index("ctx")
+    n_ctx = 2 * line_len
+    line, pair = c // 2, c % 2
+    ahead = (b, 2 * lax.rem(line + 1, line_len) + pair)
+    across, chip, core = (b, c ^ 1), (b ^ 2, c), (b ^ 1, c)
+    others = [(b, lax.rem(c + k, n_ctx)) for k in range(1, n_ctx)]
+    greet([chip, core] + others)
+    keep = pltpu.make_async_copy(columns.at[c], columns_out.at[c], own_sem)
+    keep.start()
+
+    def place(index):
+        step, side = index // 2, index % 2
+        to = lax.rem(line - 1 - step + line_len, line_len)
+        return 2 * to + (1 - pair if side == 0 else pair)
+
+    def hand(block, target, sems, index, device):
+        copy = remote(block, target.at[index], sems.at[0, index], sems.at[1, index], device)
+        copy.start()
+        return copy
+
+    on_core, on_chip, on_pair, on_line, on_columns = [], [], [], [], []
+    for index in range(n_ctx):
+        on_core.append(hand(grads.at[b ^ 3, place(index)], core_in, core_sems, index, core))
+    for k, device in enumerate(others):
+        copy = remote(
+            columns.at[device[1]],
+            columns_out.at[c],
+            column_sems.at[0, k],
+            column_sems.at[1, k],
+            device,
+        )
+        copy.start()
+        on_columns.append(copy)
+    for index in range(n_ctx):
+        on_core.append(hand(grads.at[b ^ 1, place(index)], core_in, core_sems, n_ctx + index, core))
+    for index in range(n_ctx):
+        on_core[index].wait_recv()
+        total = grads[b ^ 2, place(index)].astype(F32) + core_in[index].astype(F32)
+        chip_out[index] = total.astype(chip_out.dtype)
+        on_chip.append(hand(chip_out.at[index], chip_in, chip_sems, index, chip))
+
+    def mine(index):
+        on_core[n_ctx + index].wait_recv()
+        on_chip[index].wait_recv()
+        return (
+            grads[b, place(index)].astype(F32)
+            + core_in[n_ctx + index].astype(F32)
+            + chip_in[index].astype(F32)
+        )
+
+    for step in range(line_len):
+        pair_out[step] = mine(2 * step).astype(pair_out.dtype)
+        on_pair.append(hand(pair_out.at[step], pair_in, pair_sems, step, across))
+        total = mine(2 * step + 1)
+        on_pair[step].wait_recv()
+        total = total + pair_in[step].astype(F32)
+        if step > 0:
+            on_line[step - 1].wait_recv()
+            total = total + line_in[step - 1].astype(F32)
+        if step < line_len - 1:
+            line_out[step] = total.astype(line_out.dtype)
+            on_line.append(hand(line_out.at[step], line_in, line_sems, step, ahead))
+        else:
+            out[...] = total
+    for copy in on_columns:
+        copy.wait()
+    for copy in on_core + on_chip + on_pair + on_line:
+        copy.wait_send()
+    keep.wait()
+
+
+def collect(grads, columns, collective_id, name):
+    n_batch, n_ctx = lax.axis_size("batch"), lax.axis_size("ctx")
+    line_len = n_ctx // 2
+    block = grads.shape[2:]
+
+    def room(count):
+        return pltpu.VMEM((count,) + block, grads.dtype)
+
+    return pl.pallas_call(
+        functools.partial(collect_kernel, line_len),
+        out_shape=(
+            jax.ShapeDtypeStruct(block, F32),
+            jax.ShapeDtypeStruct(columns.shape, columns.dtype),
+        ),
+        in_specs=[IN_VMEM, ANYWHERE],
+        out_specs=(IN_VMEM, ANYWHERE),
+        scratch_shapes=[
+            room(2 * n_ctx),
+            room(n_ctx),
+            room(line_len),
+            room(line_len - 1),
+            room(n_ctx),
+            room(line_len),
+            room(line_len - 1),
+            DMA(()),
+            DMA((2, 2 * n_ctx)),
+            DMA((2, n_ctx)),
+            DMA((2, line_len)),
+            DMA((2, line_len)),
+            DMA((2, n_ctx)),
+        ],
+        compiler_params=pltpu.CompilerParams(
+            collective_id=collective_id, has_side_effects=True, vmem_limit_bytes=60 * 2**20
+        ),
+        name=name,
+    )(grads, columns)
+
+
+def swap(values, bit):
+    size = lax.axis_size("batch")
+    return lax.ppermute(values, "batch", [(i, i ^ bit) for i in range(size)])
+
+
+def by_batch(values, b, n_batch):
+    step = values.shape[1] // n_batch
+    blocks = [lax.dynamic_slice_in_dim(values, (b ^ k) * step, step, 1) for k in range(n_batch)]
+    return jnp.concatenate(blocks, axis=1)
+
+
+def sum_by_batch(block):
+    given = jnp.stack([block(1), block(3)]).astype(BF16)
+    taken = swap(given, 1).astype(F32)
+    passed = swap((block(2) + taken[1]).astype(BF16), 2)
+    return block(0) + taken[0] + passed.astype(F32)
+
+
+def vector_rows(vectors, rows, pieces):
+    laid = [
+        jnp.pad(v.reshape(pieces, 1, -1), ((0, 0), (0, 0), (0, 128 - v.shape[0] // pieces)))
+        for v in vectors
+    ]
+    return jnp.pad(jnp.concatenate(laid, axis=1), ((0, 0), (0, rows - len(vectors)), (0, 0)))
 
 
 def local(
@@ -132,30 +490,36 @@
     count, width = hidden_in.shape
     hidden_ff = gate_weight.shape[1]
 
-    vectors = lax.all_gather(
-        jnp.concatenate([attn_gain, mlp_gain, q_bias, k_bias, v_bias]), ALL, axis=0
-    ).astype(F32)
-    edges, at = [], 0
-    for part in (attn_gain, mlp_gain, q_bias, k_bias, v_bias):
-        edges.append(vectors[:, at : at + part.shape[0]].reshape(-1))
-        at += part.shape[0]
-    gain_one, gain_two, b_query, b_key, b_value = edges
-    attn_all = lax.all_gather(
-        jnp.concatenate([q_weight, k_weight, v_weight, o_weight], axis=1), ALL, axis=0, tiled=True
-    )
-    qkv_width = width + 2 * KVW
-    w_qkv, w_out = attn_all[:, :qkv_width], attn_all[:, qkv_width:]
-    b_qkv = jnp.concatenate([b_query, b_key, b_value])
+    b = lax.axis_index("batch")
+    w_down = lax.all_gather(down_weight, "batch", axis=0, tiled=True)
+    out_grad_all = lax.all_gather(out_grad, "ctx", axis=0, tiled=True)
+    rows = q_weight.shape[0]
+    small = (attn_gain, mlp_gain, q_bias, k_bias, v_bias)
+    places = (positions // 64, positions % 64, doc_ids)
+    small = vector_rows(small + tuple(row.astype(BF16) for row in places), rows, 1)[0]
+    own = jnp.concatenate([q_weight, k_weight, v_weight, o_weight, small], axis=1)
     packed = jnp.concatenate(
         [pack_columns(gate_weight, n_batch, n_ctx), pack_columns(up_weight, n_batch, n_ctx)], axis=2
     )
     half = packed.shape[2] // 2
-    packed = lax.all_to_all(packed, "ctx", split_axis=0, concat_axis=0)
-    w_gate_up = lax.all_gather(packed.reshape(-1, 2 * half), "batch", axis=0, tiled=True)
-    w_down = lax.all_gather(down_weight, "batch", axis=0, tiled=True)
+    attn_all, packed = spread(own, packed, 1, "spread_weights")
+    own_rows = packed.reshape(-1, 2 * half)
+    near, far = swap(own_rows, 1), swap(own_rows, 2)
+    w_gate_up = jnp.concatenate([own_rows, near, far, swap(far, 1)], axis=0)
+    small = attn_all[:, :, :8, own.shape[1] - 128 :].astype(F32)
+    gain_one, gain_two, b_query, b_key, b_value = (
+        small[:, :, i, : part.shape[0]].reshape(-1)
+        for i, part in enumerate((attn_gain, mlp_gain, q_bias, k_bias, v_bias))
+    )
+    places = lax.dynamic_index_in_dim(small, b, 0, keepdims=False)[:, 5:8, :count]
+    key_pos = (places[:, 0] * 64 + places[:, 1]).astype(jnp.int32).reshape(-1)
+    key_doc = places[:, 2].astype(jnp.int32).reshape(-1)
+    attn_all = attn_all.reshape(width, -1)
+    qkv_width = width + 2 * KVW
+    w_qkv, w_out = attn_all[:, :qkv_width], attn_all[:, qkv_width : qkv_width + width]
+    b_qkv = jnp.concatenate([b_query, b_key, b_value])
     own_ff = w_down.shape[0]
     w_down = jnp.pad(w_down, ((0, half - own_ff), (0, 0)))
-    out_grad_all = lax.all_gather(out_grad, "ctx", axis=0, tiled=True)
 
     cosine, sine_table = rope_tables(positions)
     hidden_wide = hidden_in.astype(F32)
@@ -167,10 +531,9 @@
     ).astype(BF16).reshape(count, width + KVW)
     query_heads = heads_of(turned[:, :width])
     key_value = jnp.concatenate([turned[:, width:], lin[:, width + KVW :].astype(BF16)], axis=1)
-    key_value = lax.all_gather(key_value, "ctx", axis=0, tiled=True)
-    places = lax.all_gather(jnp.stack([positions, doc_ids]), "ctx", axis=1, tiled=True)
+    key_value = gather_ctx(key_value, 2, "gather_keys").reshape(-1, 2 * KVW)
     key_heads, value_heads = kv_heads_of(key_value[:, :KVW]), kv_heads_of(key_value[:, KVW:])
-    allowed = (places[0][None, :] <= positions[:, None]) & (places[1][None, :] == doc_ids[:, None])
+    allowed = (key_pos[None, :] <= positions[:, None]) & (key_doc[None, :] == doc_ids[:, None])
     allowed = jnp.tile(allowed, (GROUPS, 1))
     scores = jnp.einsum("jqd,jkd->jqk", query_heads, key_heads, preferred_element_type=F32)
     scores = jnp.where(allowed[None], scores * INV_ROOT, MASKED)
@@ -182,7 +545,8 @@
     residual = hidden_wide + dot(attn_out, w_out)
 
     normed_mid, factor_two = norm_rows(residual, gain_two)
-    normed_two = lax.all_gather(normed_mid.astype(BF16), "ctx", axis=0, tiled=True)
+    normed_two = by_batch(normed_mid.astype(BF16), b, n_batch)
+    normed_two = gather_ctx(normed_two, 3, "gather_tokens").reshape(-1, width)
     gate_up = dot(normed_two, w_gate_up)
     gate_lin, up_lin = gate_up[:, :half], gate_up[:, half:]
     sigmoid_gate = jax.nn.sigmoid(gate_lin)
@@ -191,22 +555,18 @@
     d_gate = d_mixed * up_lin * sigmoid_gate * (1.0 + gate_lin * (1.0 - sigmoid_gate))
     d_up = d_mixed * (gate_lin * sigmoid_gate)
     d_gate_up = jnp.concatenate([d_gate.astype(BF16), d_up.astype(BF16)], axis=1)
-    d_normed_two = lax.psum_scatter(
-        times_transposed(d_gate_up, w_gate_up).astype(BF16), "ctx", scatter_dimension=0, tiled=True
-    ).astype(F32)
+    d_normed_two = scatter_ctx(
+        times_transposed(d_gate_up, w_gate_up).astype(BF16), 4, "scatter_tokens"
+    )
+    d_normed_two = by_batch(d_normed_two, b, n_batch)
     ff_out = lax.psum_scatter(
         dot(mixed_rows, w_down).astype(BF16), "ctx", scatter_dimension=0, tiled=True
     )
     hidden_out = (residual + ff_out.astype(F32)).astype(BF16)
-    down_grad = contract_rows(mixed_rows, out_grad_all)[:own_ff].astype(BF16)
-    down_grad = lax.psum_scatter(down_grad, "batch", scatter_dimension=0, tiled=True)
-    gate_up_grad = contract_rows(normed_two, d_gate_up).astype(BF16)
-    gate_up_grad = lax.psum_scatter(gate_up_grad, "batch", scatter_dimension=0, tiled=True)
-    gate_up_grad = lax.all_to_all(
-        gate_up_grad.reshape(n_ctx, -1, 2 * half), "ctx", split_axis=0, concat_axis=0
-    ).astype(F32)
-    gate_grad = unpack_columns(gate_up_grad[:, :, :half], n_batch, hidden_ff)
-    up_grad = unpack_columns(gate_up_grad[:, :, half:], n_batch, hidden_ff)
+    down_grad_all = contract_rows(mixed_rows, out_grad_all)[:own_ff].reshape(n_batch, -1, width)
+    down_grad = sum_by_batch(lambda k: lax.dynamic_index_in_dim(down_grad_all, b ^ k, 0, False))
+    gate_up_grad_all = contract_rows(normed_two, d_gate_up).reshape(n_batch, -1, 2 * half)
+    gate_up_grad = sum_by_batch(lambda k: gate_up_grad_all[k]).astype(BF16)
 
     d_residual_norm, gain_two_grad = norm_back(residual, factor_two, gain_two, d_normed_two)
     d_residual = out_grad.astype(F32) + d_residual_norm
@@ -222,9 +582,7 @@
     d_keys = jnp.einsum("jqk,jqd->kjd", d_scores, query_heads, preferred_element_type=F32) * INV_ROOT
     d_values = jnp.einsum("jqk,jqd->kjd", attn_probs, grad_heads, preferred_element_type=F32)
     d_key_value = jnp.concatenate([d_keys.reshape(-1, KVW), d_values.reshape(-1, KVW)], axis=1)
-    d_key_value = lax.psum_scatter(
-        d_key_value.astype(BF16), "ctx", scatter_dimension=0, tiled=True
-    ).astype(F32)
+    d_key_value = scatter_ctx(d_key_value.astype(BF16), 5, "scatter_keys")
     d_turned = jnp.concatenate([d_queries, d_key_value[:, :KVW]], axis=1)
     d_turned = rotate_back(
         d_turned.reshape(count, HEADS + KV_HEADS, HEAD_DIM), cosine, sine_table
@@ -236,25 +594,48 @@
     d_hidden_norm, gain_one_grad = norm_back(hidden_wide, factor_one, gain_one, d_normed_one)
     hidden_grad = d_residual + d_hidden_norm
 
-    attn_grads = jnp.concatenate([qkv_grad.astype(BF16), out_proj_grad.astype(BF16)], axis=1)
-    attn_grads = lax.psum_scatter(attn_grads, ALL, scatter_dimension=0, tiled=True).astype(F32)
-    sums = lax.psum(jnp.concatenate([gain_one_grad, bias_grad, gain_two_grad]), ALL)
+    sums = (
+        gain_one_grad,
+        gain_two_grad,
+        bias_grad[:width],
+        bias_grad[width : width + KVW],
+        bias_grad[width + KVW :],
+    )
+    attn_grads = jnp.concatenate(
+        [
+            qkv_grad.astype(BF16).reshape(n_all, rows, -1),
+            out_proj_grad.astype(BF16).reshape(n_all, rows, -1),
+            vector_rows(sums, rows, n_all).astype(BF16),
+        ],
+        axis=2,
+    ).reshape(n_batch, n_ctx, rows, -1)
+    attn_grads, gate_up_grad = collect(
+        attn_grads, gate_up_grad.reshape(n_ctx, rows, -1), 6, "collect_grads"
+    )
+    gate_up_grad = gate_up_grad.astype(F32)
+    gate_grad = unpack_columns(gate_up_grad[:, :, :half], n_batch, hidden_ff)
+    up_grad = unpack_columns(gate_up_grad[:, :, half:], n_batch, hidden_ff)
+    sums = attn_grads[:8, own.shape[1] - 128 :]
+    gain_one_grad, gain_two_grad, query_bias_grad, key_bias_grad, value_bias_grad = (
+        sums[i, : part.shape[0]]
+        for i, part in enumerate((attn_gain, mlp_gain, q_bias, k_bias, v_bias))
+    )
     at_key, at_value, at_out = width, width + KVW, width + 2 * KVW
     return (
         hidden_out,
         hidden_grad,
-        own_slice(sums[:width]),
+        gain_one_grad,
         attn_grads[:, :at_key],
-        own_slice(sums[width : 2 * width]),
+        query_bias_grad,
         attn_grads[:, at_key:at_value],
-        own_slice(sums[2 * width : 2 * width + KVW]),
+        key_bias_grad,
         attn_grads[:, at_value:at_out],
-        own_slice(sums[2 * width + KVW : 2 * width + 2 * KVW]),
-        attn_grads[:, at_out:],
-        own_slice(sums[2 * width + 2 * KVW :]),
+        value_bias_grad,
+        attn_grads[:, at_out : at_out + width],
+        gain_two_grad,
         gate_grad,
         up_grad,
-        lax.convert_element_type(down_grad, F32),
+        down_grad,
     )
 
 

time: 928 us -> 559 us (0.60)
  waiting for transfers between devices: 549 us -> 0.75 us
  Pallas kernels: 0 us -> 312 us
  blocking collectives: 139 us -> 0 us
  other arithmetic: 32.6 us -> 49.8 us
  starting transfers between devices: 13.7 us -> 3.09 us
    pallas_call x0 -> x6, Pallas kernels: none -> 312 us  [the longest x2 84.2 us: scatter_ctx(): pl.pallas_call(functools.partial(scatter_kernel, line_len), out_shape=jax...]
    reduce_scatter x4 -> x0, waiting for transfers between devices: 230 us -> none  [the longest x1 76.5 us: local(): lax.psum_scatter(attn_grads, ALL, scatter_dimension=0, tiled=True)]
    all_gather x4 -> x0, waiting for transfers between devices: 130 us -> none  [the longest x1 63.1 us: local(): lax.all_gather(normed_mid.astype(BF16), 'ctx', axis=0, tiled=True)]
    unnamed x1 -> x0, blocking collectives: 79.9 us -> none
    reduce_scatter x1, waiting for transfers between devices: 75.8 us -> 0.01 us  [local(): lax.psum_scatter(dot(mixed_rows, w_down).astype(BF16), 'ctx', scatter_dim...]
    all_gather x1, waiting for transfers between devices: 62.5 us -> 0.01 us  [local(): out_grad_all = lax.all_gather(out_grad, 'ctx', axis=0, tiled=True)]
    psum x1 -> x0, blocking collectives: 39.8 us -> none  [local(): lax.psum(jnp.concatenate([gain_one_grad, bias_grad, gain_two_grad]), ALL)]
    unnamed x13 -> x3, waiting for transfers between devices: 33.7 us -> 0.71 us
  transfers between devices with their start and end apart: 14 -> 10, of which waited for: 12 -> 0; matrix products, arithmetic and copies ran while one was open for 16% -> 19% of each run, Pallas kernels for 0% -> 39%
where the time goes in v2:
time: 559 us; the launch traced here: 550 us
  Pallas kernels  312 us (56%)
  matrix products  100 us (18%)
  local copies, waits for them, and re-layouts  68 us (12%)
  other arithmetic  49.8 us (9%)
  between operations  15.4 us (3%)
    pallas_call x2, Pallas kernels, scatter_ctx(): pl.pallas_call(functools.partial(scatter_kernel, line_len), out_shape=jax...  84.2 us
    pallas_call x2, Pallas kernels, gather_ctx(): pl.pallas_call(functools.partial(gather_kernel, line_len), out_shape=jax....  79.5 us
    pallas_call x1, Pallas kernels, spread(): pl.pallas_call(functools.partial(spread_kernel, line_len), out_shape=(jax...  76.2 us
    pallas_call x1, Pallas kernels, collect(): pl.pallas_call(functools.partial(collect_kernel, line_len), out_shape=(ja...  72.6 us
    dot_general x4, matrix products, times_transposed(): lax.dot_general(lhs, rhs, (((1,), (1,)), ((), ())), preferred_element_typ...  34.3 us
    dot_general x4, matrix products, dot(): return jnp.dot(lhs, rhs, preferred_element_type=F32)  26.6 us
    dot_general x4, matrix products, contract_rows(): lax.dot_general(lhs, rhs, (((0,), (0,)), ((), ())), preferred_element_typ...  22.8 us
    unnamed x119, local copies, waits for them, and re-layouts  11.5 us
  transfers between devices with their start and end apart: 10, of which 0 were waited for; matrix products, arithmetic and copies ran while one was open for 19% of the time, Pallas kernels for 39%

profile of v2, /device:TPU:0, one launch (start us, length us, event | category | flops | bytes accessed | tf_op | source)
XLA Modules:
  0.0 549.8 jit_solution(11716003798670979961)
XLA Ops:
  17.6 3.6 reshape.387
  28.4 76.2 %spread_weights.1 = (bf16[4,8,48,3712]{3,2,1,0:T(8,128)(2,1)}, bf16[8,48,2304]{2,1,0:T(8,128)(2,1)}) custom-call(bf16[48,3712]{1,0:T(8,128)(2,1)} %copy-done.25, bf16[8,48,2304]{2,1,0:T(8,128)(2,1)} %fusion.40.columns), custom_call_target="tpu_custom_call" | custom-call | tf_op jit(solution)/shard_map/spread_weights/pallas_call | solution.py:310
  107.5 3.8 fusion.32
  116.1 34.5 %gather_keys.1 = bf16[8,128,512]{2,1,0:T(8,128)(2,1)} custom-call(bf16[128,512]{1,0:T(8,128)(2,1)} %pad_maximum_fusion.17.own), custom_call_target="tpu_custom_call" | custom-call | tf_op jit(solution)/shard_map/gather_keys/pallas_call | solution.py:164
  153.4 4.9 fusion.106
  158.4 3.8 fusion.52
  168.0 45.0 %gather_tokens.1 = bf16[8,128,1536]{2,1,0:T(8,128)(2,1)} custom-call(bf16[128,1536]{1,0:T(8,128)(2,1)} %pad_maximum_fusion.14.own), custom_call_target="tpu_custom_call" | custom-call | tf_op jit(solution)/shard_map/gather_tokens/pallas_call | solution.py:164
  213.1 13.6 %fusion.55 = f32[1024,2304]{1,0:T(8,128)} fusion(bf16[1024,1536]{1,0:T(8,128)(2,1)} %bitcast.180, bf16[384,2304]{1,0:T(8,128)(2,1)} %collective-permute-done.2, bf16[384,2304]{1,0:T(8,128)(2,1)} %collective-permute-done.1, bf16[384,2304]{1,0:T(8,128)(2,1)} %collective-permute-done, bf16[384,2304]{1,0:T(8,128)(2,1)S(1)} %bitcast.210), kind=kOutput, calls=%fused_computation.80 | convolution fusion | flops 7276068864 | bytes 19660800 | tf_op jit(solution)/shard_map/dot_general | solution.py:67
  226.7 11.3 %fusion.8 = (bf16[1024,1152]{1,0:T(8,128)(2,1)S(1)}, bf16[1024,1152]{1,0:T(8,128)(2,1)S(1)}, bf16[1024,1152]{1,0:T(8,128)(2,1)S(1)}) fusion(f32[1024,2304]{1,0:T(8,128)} %fusion.55, bf16[1024,1536]{1,0:T(8,128)(2,1)} %all-gather.5.cloned.1.call-done, bf16[1120,1536]{1,0:T(8,128)(2,1)} %all-gather.3.cloned.1.call-done), kind=kOutput, calls=%fused_computation.19 | convolution fusion | flops 3641573376 | bytes 23101440 | tf_op jit(solution)/shard_map/dot_general | solution.py:75
  238.0 10.8 %fusion.111 = (bf16[1536,2304]{1,0:T(8,128)(2,1)S(1)}, f32[1536,2304]{1,0:T(8,128)}) fusion(bf16[1024,1536]{1,0:T(8,128)(2,1)S(1)} %bitcast.181, bf16[1024,1152]{1,0:T(8,128)(2,1)S(1)} %get-tuple-element.32, bf16[1024,1152]{1,0:T(8,128)(2,1)S(1)} %get-tuple-element.31), kind=kOutput, calls=%fused_computation.199 | convolution fusion | flops 7260733440 | bytes 29097984 | tf_op jit(solution)/shard_map/dot_general | solution.py:71
  252.3 3.8 fusion.38
  260.6 5.7 %convolution_convert_fusion.3 = bf16[1024,1536]{1,0:T(8,128)(2,1)} fusion(bf16[1024,1152]{1,0:T(8,128)(2,1)S(1)} %get-tuple-element.33, bf16[1120,1536]{1,0:T(8,128)(2,1)S(1)} %copy-done.44), kind=kOutput, calls=%fused_computation.29 | convolution fusion | flops 3625451520 | bytes 8945664 | tf_op jit(solution)/shard_map/dot_general | solution.py:67
  274.5 6.3 %fusion.16 = bf16[384,2304]{1,0:T(8,128)(2,1)} fusion(f32[2,384,2304]{2,1,0:T(8,128)S(1)} %convert_element_type.194, f32[1536,2304]{1,0:T(8,128)} %get-tuple-element.86), kind=kLoop, calls=%fused_computation.32 | loop fusion | flops 1769472 | bytes 8847360 | tf_op jit(solution)/shard_map/convert_element_type | solution.py:458
  281.8 12.3 %convolution_convert_fusion.2 = bf16[1024,1536]{1,0:T(8,128)(2,1)} fusion(bf16[1024,1152]{1,0:T(8,128)(2,1)} %copy-done.50, bf16[1024,1152]{1,0:T(8,128)(2,1)S(1)} %copy-done.49, bf16[384,2304]{1,0:T(8,128)(2,1)} %collective-permute-done.2, bf16[384,2304]{1,0:T(8,128)(2,1)} %collective-permute-done.1, bf16[384,2304]{1,0:T(8,128)(2,1)} %collective-permute-done, ...), kind=kOutput, calls=%fused_computation.28 | convolution fusion | flops 7287078912 | bytes 14942208 | tf_op jit(solution)/shard_map/dot_general | solution.py:75
  294.1 60.2 %scatter_tokens.1 = f32[128,1536]{1,0:T(8,128)} custom-call(bf16[8,128,1536]{2,1,0:T(8,128)(2,1)} %bitcast.182), custom_call_target="tpu_custom_call" | custom-call | tf_op jit(solution)/shard_map/scatter_tokens/pallas_call | solution.py:224
  359.8 5.4 fusion.19
  367.4 4.8 fusion.35
  372.2 3.6 convolution_convert_fusion.1
  377.9 3.9 fusion.48
  392.4 24.0 %scatter_keys.1 = f32[128,512]{1,0:T(8,128)} custom-call(bf16[8,128,512]{2,1,0:T(8,128)(2,1)} %pad_maximum_fusion.9.parts), custom_call_target="tpu_custom_call" | custom-call | tf_op jit(solution)/shard_map/scatter_keys/pallas_call | solution.py:224
  419.8 5.9 %fusion.66 = (bf16[1536]{0:T(1024)(128)(2,1)S(1)}, f32[128]{0:T(128)S(1)}, f32[128,1536]{1,0:T(8,128)}) fusion(bf16[128,1536]{1,0:T(8,128)(2,1)S(1)} %copy-done.5, f32[128]{0:T(128)S(1)} %copy-done.38, f32[1536]{0:T(1024)S(1)} %copy-done.36, bf16[1536,3712]{1,0:T(8,128)(2,1)} %bitcast.207, bf16[128,256]{0,1:T(8,128)(2,1)S(1)} %copy.63, ...), kind=kOutput, calls=%fused_computation.99 | convolution fusion | flops 807729536 | bytes 8005632 | tf_op jit(solution)/shard_map/dot_general | solution.py:75
  426.0 4.5 convolution_convert_fusion
  431.0 9.7 %pad_maximum_fusion.grads = bf16[4,8,48,3712]{3,2,1,0:T(8,128)(2,1)} fusion(bf16[4,8,48,128]{3,2,1,0:T(8,128)(2,1)S(1)} %bitcast.195, bf16[4,8,48,1536]{3,2,1,0:T(8,128)(2,1)} %bitcast.162, bf16[4,8,48,2048]{3,2,1,0:T(8,128)(2,1)} %bitcast.161), kind=kLoop, calls=%fused_computation.1 | loop fusion | flops 34209792 | bytes 22806528 | tf_op jit(solution)/shard_map/concatenate | solution.py:604
  440.7 72.6 %collect_grads.1 = (f32[48,3712]{1,0:T(8,128)}, bf16[8,48,2304]{2,1,0:T(8,128)(2,1)}) custom-call(bf16[4,8,48,3712]{3,2,1,0:T(8,128)(2,1)} %pad_maximum_fusion.grads, bf16[8,48,2304]{2,1,0:T(8,128)(2,1)} %bitcast.167), custom_call_target="tpu_custom_call" | custom-call | tf_op jit(solution)/shard_map/collect_grads/pallas_call | solution.py:414
  (252 shorter events, 104.1 us)
Async XLA Ops:
  7.2 219.5 %all-gather.3.cloned.1.call-start = ((), (), s32[]{:S(2)}) async-start(), calls=%async_computation.1 | async-start | bytes 4300800 | tf_op jit(solution)/shard_map/all_gather | solution.py:494
  7.9 218.8 %all-gather.5.cloned.1.call-start = ((), (), s32[]{:S(2)}) async-start(), calls=%async_computation.3 | async-start | bytes 3538944 | tf_op jit(solution)/shard_map/all_gather | solution.py:495
  17.6 6.6 %copy-start.33 = (bf16[48,1536]{1,0:T(8,128)(2,1)S(1)}, bf16[48,1536]{1,0:T(8,128)(2,1)}, u32[]{:S(2)}) copy-start(bf16[48,1536]{1,0:T(8,128)(2,1)} %param.20) | copy-start | bytes 442372
  17.6 8.1 %copy-start.34 = (bf16[48,1536]{1,0:T(8,128)(2,1)S(1)}, bf16[48,1536]{1,0:T(8,128)(2,1)}, u32[]{:S(2)}) copy-start(bf16[48,1536]{1,0:T(8,128)(2,1)} %param.26) | copy-start | bytes 442372
  24.2 82.3 %copy-start.4 = (bf16[128,1536]{1,0:T(8,128)(2,1)S(1)}, bf16[128,1536]{1,0:T(8,128)(2,1)}, u32[]{:S(2)}) copy-start(bf16[128,1536]{1,0:T(8,128)(2,1)} %param.16) | copy-start | bytes 1179652
  104.6 53.8 %collective-permute-start.1 = (bf16[384,2304]{1,0:T(8,128)(2,1)}, bf16[384,2304]{1,0:T(8,128)(2,1)}, u32[]{:S(2)}, u32[]{:S(2)}) collective-permute-start(bf16[384,2304]{1,0:T(8,128)(2,1)} %bitcast.208), channel_id=1, source_target_pairs={{0,16},{8,24},{16,0},{24,8},{1,17},{9,25},{17,1},{25,9},{2,18},{10... | collective-permute-start | bytes 5308424 | tf_op jit(solution)/shard_map/ppermute | solution.py:446
  105.0 108.1 %collective-permute-start = (bf16[384,2304]{1,0:T(8,128)(2,1)}, bf16[384,2304]{1,0:T(8,128)(2,1)}, u32[]{:S(2)}, u32[]{:S(2)}) collective-permute-start(bf16[384,2304]{1,0:T(8,128)(2,1)} %bitcast.209), channel_id=1, source_target_pairs={{0,8},{8,0},{16,24},{24,16},{1,9},{9,1},{17,25},{25,17},{2,10},{10... | collective-permute-start | bytes 5308424 | tf_op jit(solution)/shard_map/ppermute | solution.py:446
  105.1 260.2 %reduce-scatter.2.cloned.1.call-start = ((), (), s32[]{:S(2)}) async-start(), calls=%async_computation.2 | async-start | bytes 3538944 | tf_op jit(solution)/shard_map/reduce_scatter | solution.py:562
  115.4 38.0 %copy-start.22 = (bf16[2,6,128,128]{3,2,1,0:T(8,128)(2,1)}, bf16[2,6,128,128]{3,2,1,0:T(8,128)(2,1)S(1)}, u32[]{:S(2)}) copy-start(bf16[2,6,128,128]{3,2,1,0:T(8,128)(2,1)S(1)} %copy.48) | copy-start | bytes 1179652
  158.4 54.7 %collective-permute-start.2 = (bf16[384,2304]{1,0:T(8,128)(2,1)}, bf16[384,2304]{1,0:T(8,128)(2,1)}, u32[]{:S(2)}, u32[]{:S(2)}) collective-permute-start(bf16[384,2304]{1,0:T(8,128)(2,1)} %collective-permute-done.1), channel_id=1, source_target_pairs={{0,8},{8,0},{16,24},{24,16},{1,9},{9,1},{17,25},{25,17},{2,10},{10... | collective-permute-start | bytes 5308424 | tf_op jit(solution)/shard_map/ppermute | solution.py:446
  166.2 46.9 %copy-start.46 = (bf16[8,48,2304]{2,1,0:T(8,128)(2,1)S(1)}, bf16[8,48,2304]{2,1,0:T(8,128)(2,1)}, u32[]{:S(2)}) copy-start(bf16[8,48,2304]{2,1,0:T(8,128)(2,1)} %get-tuple-element.19) | copy-start | bytes 5308420
  226.7 11.3 %copy-start.8 = (bf16[8,128,1536]{2,1,0:T(8,128)(2,1)S(1)}, bf16[8,128,1536]{2,1,0:T(8,128)(2,1)}, u32[]{:S(2)}) copy-start(bf16[8,128,1536]{2,1,0:T(8,128)(2,1)} %gather_tokens.1) | copy-start | bytes 9437188
  238.0 10.9 %copy-start.48 = (bf16[1024,1152]{1,0:T(8,128)(2,1)}, bf16[1024,1152]{1,0:T(8,128)(2,1)S(1)}, u32[]{:S(2)}) copy-start(bf16[1024,1152]{1,0:T(8,128)(2,1)S(1)} %get-tuple-element.31) | copy-start | bytes 7077892
  238.0 10.9 %copy-start.50 = (bf16[1024,1152]{1,0:T(8,128)(2,1)}, bf16[1024,1152]{1,0:T(8,128)(2,1)S(1)}, u32[]{:S(2)}) copy-start(bf16[1024,1152]{1,0:T(8,128)(2,1)S(1)} %get-tuple-element.32) | copy-start | bytes 7077892
  251.2 20.7 %collective-permute-start.3 = (bf16[2,384,2304]{2,1,0:T(8,128)(2,1)}, bf16[2,384,2304]{2,1,0:T(8,128)(2,1)}, u32[]{:S(2)}, u32[]{:S(2)}) collective-permute-start(bf16[2,384,2304]{2,1,0:T(8,128)(2,1)} %pad_maximum_fusion.3), channel_id=1, source_target_pairs={{0,8},{8,0},{16,24},{24,16},{1,9},{9,1},{17,25},{25,17},{2,10},{10... | collective-permute-start | bytes 10616840 | tf_op jit(solution)/shard_map/ppermute | solution.py:446
  260.0 6.3 %collective-permute-start.5 = (bf16[2,280,1536]{2,1,0:T(8,128)(2,1)S(1)}, bf16[2,280,1536]{2,1,0:T(8,128)(2,1)}, u32[]{:S(2)}, u32[]{:S(2)}) collective-permute-start(bf16[2,280,1536]{2,1,0:T(8,128)(2,1)S(1)} %pad_maximum_fusion.6), channel_id=1, source_target_pairs={{0,8},{8,0},{16,24},{24,16},{1,9},{9,1},{17,25},{25,17},{2,10},{10... | collective-permute-start | bytes 5160968 | tf_op jit(solution)/shard_map/ppermute | solution.py:446
  270.8 85.8 %collective-permute-start.6 = (bf16[280,1536]{1,0:T(8,128)(2,1)}, bf16[280,1536]{1,0:T(8,128)(2,1)}, u32[]{:S(2)}, u32[]{:S(2)}) collective-permute-start(bf16[280,1536]{1,0:T(8,128)(2,1)} %fusion.57), channel_id=1, source_target_pairs={{0,16},{8,24},{16,0},{24,8},{1,17},{9,25},{17,1},{25,9},{2,18},{10... | collective-permute-start | bytes 2580488 | tf_op jit(solution)/shard_map/ppermute | solution.py:446
  274.5 7.3 %copy-start.47 = (bf16[8,48,2304]{2,1,0:T(8,128)(2,1)S(1)}, bf16[8,48,2304]{2,1,0:T(8,128)(2,1)}, u32[]{:S(2)}) copy-start(bf16[8,48,2304]{2,1,0:T(8,128)(2,1)} %get-tuple-element.19) | copy-start | bytes 5308420
  274.5 7.3 %copy-start.49 = (bf16[1024,1152]{1,0:T(8,128)(2,1)S(1)}, bf16[1024,1152]{1,0:T(8,128)(2,1)}, u32[]{:S(2)}) copy-start(bf16[1024,1152]{1,0:T(8,128)(2,1)} %copy-done.48) | copy-start | bytes 7077892
  280.8 79.1 %collective-permute-start.4 = (bf16[384,2304]{1,0:T(8,128)(2,1)}, bf16[384,2304]{1,0:T(8,128)(2,1)}, u32[]{:S(2)}, u32[]{:S(2)}) collective-permute-start(bf16[384,2304]{1,0:T(8,128)(2,1)} %fusion.16), channel_id=1, source_target_pairs={{0,16},{8,24},{16,0},{24,8},{1,17},{9,25},{17,1},{25,9},{2,18},{10... | collective-permute-start | bytes 5308424 | tf_op jit(solution)/shard_map/ppermute | solution.py:446
  294.1 61.6 %copy-start.2 = (f32[128,1536]{1,0:T(8,128)S(1)}, f32[128,1536]{1,0:T(8,128)}, u32[]{:S(2)}) copy-start(f32[128,1536]{1,0:T(8,128)} %copy-done.1) | copy-start | bytes 2359300
  372.2 9.7 %slice-start = ((s8[6291456]{0:T(1024)(128)(4,1)}), s8[2097152]{0:T(1024)(128)(4,1)S(1)}, s32[]{:S(2)}) async-start(s8[6291456]{0:T(1024)(128)(4,1)} %bitcast.168), calls=%async_computation.4 | async-start | bytes 4194304
  390.3 28.5 %copy-start.29 = (f32[128,128]{0,1:T(8,128)S(1)}, f32[128,128]{0,1:T(8,128)}, u32[]{:S(2)}) copy-start(f32[128,128]{0,1:T(8,128)} %copy-done.28) | copy-start | bytes 196612
  535.2 6.3 %copy-start.39 = (f32[128]{0:T(128)S(1)}, f32[128]{0:T(128)}, u32[]{:S(2)}) copy-start(f32[128]{0:T(128)} %copy-done.37) | copy-start | bytes 1540
  (39 other events, 133.1 us)
Sparse Core Ops, SparseCore 0:
  9.6 37.0 all-gather.2
  105.2 68.5 all-gather.4
  266.4 90.3 reduce-scatter.1

commit v3 on v2

v3 whole, which is shorter than its diff:
```python
import functools
import math

import jax
import jax.numpy as jnp
from jax import lax
from jax.experimental import pallas as pl
from jax.experimental.pallas import tpu as pltpu
from jax.sharding import PartitionSpec as P

HEADS = 12
KV_HEADS = 2
GROUPS = HEADS // KV_HEADS
HEAD_DIM = 128
KVW = KV_HEADS * HEAD_DIM
INV_ROOT = HEAD_DIM ** (-0.5)
EPSILON = 1e-06
ROPE_BASE = 10000.0
MASKED = -1e30
ALL = ("batch", "ctx")
F32 = jnp.float32
BF16 = jnp.bfloat16
MESH = pl.DeviceIdType.MESH
ANYWHERE = pl.BlockSpec(memory_space=pl.ANY)
IN_VMEM = pl.BlockSpec(memory_space=pltpu.VMEM)
DMA = pltpu.SemaphoreType.DMA


def rope_tables(positions):
    half_dim = HEAD_DIM // 2
    inverse_freq = jnp.exp(
        jnp.arange(half_dim, dtype=F32) * (-2.0 * math.log(ROPE_BASE) / HEAD_DIM)
    )
    angles = positions.astype(F32)[:, None] * inverse_freq[None, :]
    angles = jnp.concatenate([angles, angles], axis=1)
    return (jnp.cos(angles), jnp.sin(angles))


def dot(lhs, rhs):
    return jnp.dot(lhs, rhs, preferred_element_type=F32)


def contract_rows(lhs, rhs):
    return lax.dot_general(lhs, rhs, (((0,), (0,)), ((), ())), preferred_element_type=F32)


def times_transposed(lhs, rhs):
    return lax.dot_general(lhs, rhs, (((1,), (1,)), ((), ())), preferred_element_type=F32)


def lanes(width):
    return -(-width // 128) * 128


def greet(devices):
    barrier = pltpu.get_barrier_semaphore()
    for device in devices:
        pl.semaphore_signal(barrier, inc=1, device_id=device, device_id_type=MESH)
    pl.semaphore_wait(barrier, len(devices))


def remote(source, target, send, receive, device):
    return pltpu.make_async_remote_copy(
        src_ref=source,
        dst_ref=target,
        send_sem=send,
        recv_sem=receive,
        device_id=device,
        device_id_type=MESH,
    )


def lasting(microseconds):
    return pl.CostEstimate(flops=0, bytes_accessed=int(3.3e6 * microseconds), transcendentals=0)


def gather_kernel(line_len, own, out, own_sem, line_sems, pair_sems):
    b, c = lax.axis_index("batch"), lax.axis_index("ctx")
    line, pair = c // 2, c % 2
    ahead = (b, 2 * lax.rem(line + 1, line_len) + pair)
    behind = (b, 2 * lax.rem(line + line_len - 1, line_len) + pair)
    across = (b, c ^ 1)
    greet((ahead, behind, across))
    keep = pltpu.make_async_copy(own, out.at[c], own_sem)
    keep.start()
    on_line, on_pair = [], []
    for step in range(line_len):
        at = 2 * lax.rem(line - step + line_len, line_len) + pair
        block = own if step == 0 else out.at[at]
        if step > 0:
            on_line[step - 1].wait_recv()
        if step < line_len - 1:
            copy = remote(block, out.at[at], line_sems.at[0, step], line_sems.at[1, step], ahead)
            copy.start()
            on_line.append(copy)
        copy = remote(block, out.at[at], pair_sems.at[0, step], pair_sems.at[1, step], across)
        copy.start()
        on_pair.append(copy)
    for copy in on_pair:
        copy.wait()
    for copy in on_line:
        copy.wait_send()
    keep.wait()


def gather_ctx(block, collective_id, name):
    n_ctx = lax.axis_size("ctx")
    line_len = n_ctx // 2
    return pl.pallas_call(
        functools.partial(gather_kernel, line_len),
        out_shape=jax.ShapeDtypeStruct((n_ctx,) + block.shape, block.dtype),
        in_specs=[ANYWHERE],
        out_specs=ANYWHERE,
        scratch_shapes=[DMA(()), DMA((2, line_len)), DMA((2, line_len))],
        compiler_params=pltpu.CompilerParams(collective_id=collective_id, has_side_effects=True),
        cost_estimate=lasting(20),
        name=name,
    )(block)


def scatter_kernel(line_len, many, *refs):
    parts, outs = refs[:many], refs[many : 2 * many]
    pair_in, line_in, line_out = (refs[(2 + i) * many : (3 + i) * many] for i in range(3))
    pair_sems, line_sems = refs[5 * many :]
    b, c = lax.axis_index("batch"), lax.axis_index("ctx")
    line, pair = c // 2, c % 2
    ahead = (b, 2 * lax.rem(line + 1, line_len) + pair)
    behind = (b, 2 * lax.rem(line + line_len - 1, line_len) + pair)
    across = (b, c ^ 1)
    greet((ahead, behind, across))

    def to(step):
        return 2 * lax.rem(line - 1 - step + line_len, line_len)

    sent, given = [], []
    for i in range(many):
        for step in range(line_len):
            copy = remote(
                parts[i].at[to(step) + 1 - pair],
                pair_in[i].at[step],
                pair_sems.at[0, i, step],
                pair_sems.at[1, i, step],
                across,
            )
            copy.start()
            given.append(copy)
    for i in range(many):
        for step in range(line_len):
            given[i * line_len + step].wait_recv()
            total = parts[i][to(step) + pair].astype(F32) + pair_in[i][step].astype(F32)
            if step > 0:
                passed.wait_recv()
                total = total + line_in[i][step - 1].astype(F32)
            if step < line_len - 1:
                line_out[i][step] = total.astype(BF16)
                passed = remote(
                    line_out[i].at[step],
                    line_in[i].at[step],
                    line_sems.at[0, i, step],
                    line_sems.at[1, i, step],
                    ahead,
                )
                passed.start()
                sent.append(passed)
            else:
                outs[i][...] = total
    for copy in given + sent:
        copy.wait_send()


def scatter_ctx(parts, collective_id, name):
    n_ctx = lax.axis_size("ctx")
    line_len, many = n_ctx // 2, len(parts)
    blocks = [(part.shape[0] // n_ctx,) + part.shape[1:] for part in parts]

    def room(size):
        return [pltpu.VMEM((size,) + block, BF16) for block in blocks]

    return pl.pallas_call(
        functools.partial(scatter_kernel, line_len, many),
        out_shape=[jax.ShapeDtypeStruct(block, F32) for block in blocks],
        in_specs=[IN_VMEM] * many,
        out_specs=[IN_VMEM] * many,
        scratch_shapes=[
            *room(line_len),
            *room(line_len - 1),
            *room(line_len - 1),
            DMA((2, many, line_len)),
            DMA((2, many, line_len)),
        ],
        compiler_params=pltpu.CompilerParams(
            collective_id=collective_id, has_side_effects=True, vmem_limit_bytes=60 * 2**20
        ),
        cost_estimate=lasting(40),
        name=name,
    )(*[part.reshape((n_ctx,) + block) for part, block in zip(parts, blocks)])


def spread_kernel(
    line_len, q_weight, k_weight, v_weight, o_weight, small, gate, up, out, columns_out, own,
    columns, own_sem, line_sems, pair_sems, chip_sems, core_sems, column_sems,
):
    b, c = lax.axis_index("batch"), lax.axis_index("ctx")
    n_ctx = 2 * line_len
    line, pair = c // 2, c % 2
    ahead = (b, 2 * lax.rem(line + 1, line_len) + pair)
    across, chip, core = (b, c ^ 1), (b ^ 2, c), (b ^ 1, c)
    others = [(b, lax.rem(c + k, n_ctx)) for k in range(1, n_ctx)]
    at = 0
    for part in (q_weight, k_weight, v_weight, o_weight, small):
        own[:, at : at + part.shape[1]] = part[...]
        at += part.shape[1]
    greet([chip, core] + others)
    keep = [pltpu.make_async_copy(own, out.at[b, c], own_sem.at[0])]
    keep[0].start()

    def pack():
        n_batch, half = out.shape[0], columns.shape[2] // 2
        piece = gate.shape[1] // (n_batch * n_ctx)
        for first, weight in ((0, gate), (half, up)):
            if n_batch * piece < half:
                columns[:, :, first + half - 128 : first + half] = jnp.zeros(
                    (n_ctx, columns.shape[1], 128), BF16
                )
            for k in range(n_batch):
                for i in range(n_ctx):
                    to = (k * n_ctx + i) * piece
                    at = first + k * piece
                    columns[i, :, at : at + piece] = weight[:, to : to + piece]
        keep.append(pltpu.make_async_copy(columns.at[c], columns_out.at[c], own_sem.at[1]))
        keep[1].start()

    def place(step, side):
        return 2 * lax.rem(line - step + line_len, line_len) + side

    def hand(block, to_b, to_c, sems, index, device):
        copy = remote(block, out.at[to_b, to_c], sems.at[0, index], sems.at[1, index], device)
        copy.start()
        return copy

    on_line, on_pair, on_chip, on_core, on_columns = [], [], [], [], []
    for step in range(line_len):
        at = place(step, pair)
        block = own if step == 0 else out.at[b, at]
        if step > 0:
            on_line[step - 1].wait_recv()
        if step < line_len - 1:
            on_line.append(hand(block, b, at, line_sems, step, ahead))
        on_pair.append(hand(block, b, at, pair_sems, step, across))
        on_chip.append(hand(block, b, at, chip_sems, step, chip))
        on_core.append(hand(block, b, at, core_sems, step, core))
        if step == 0:
            pack()
    for k, device in enumerate(others):
        copy = remote(
            columns.at[device[1]],
            columns_out.at[c],
            column_sems.at[0, k],
            column_sems.at[1, k],
            device,
        )
        copy.start()
        on_columns.append(copy)
    for step in range(line_len):
        at = place(step, 1 - pair)
        on_pair[step].wait_recv()
        on_chip.append(hand(out.at[b, at], b, at, chip_sems, line_len + step, chip))
        on_core.append(hand(out.at[b, at], b, at, core_sems, line_len + step, core))
    for index in range(n_ctx):
        at = place(index % line_len, pair if index < line_len else 1 - pair)
        on_chip[index].wait_recv()
        on_core.append(hand(out.at[b ^ 2, at], b ^ 2, at, core_sems, n_ctx + index, core))
    for copy in on_core + on_columns:
        copy.wait()
    for copy in on_line + on_pair + on_chip:
        copy.wait_send()
    for copy in keep:
        copy.wait()


def spread(matrices, gate, up, collective_id, name):
    n_batch, n_ctx = lax.axis_size("batch"), lax.axis_size("ctx")
    line_len = n_ctx // 2
    rows = gate.shape[0]
    own = (rows, sum(matrix.shape[1] for matrix in matrices))
    columns = (n_ctx, rows, 2 * lanes(gate.shape[1] // n_ctx))
    return pl.pallas_call(
        functools.partial(spread_kernel, line_len),
        out_shape=(
            jax.ShapeDtypeStruct((n_batch, n_ctx) + own, BF16),
            jax.ShapeDtypeStruct(columns, BF16),
        ),
        in_specs=[IN_VMEM] * 7,
        out_specs=(ANYWHERE, ANYWHERE),
        scratch_shapes=[
            pltpu.VMEM(own, BF16),
            pltpu.VMEM(columns, BF16),
            DMA((2,)),
            DMA((2, line_len)),
            DMA((2, line_len)),
            DMA((2, n_ctx)),
            DMA((2, 2 * n_ctx)),
            DMA((2, n_ctx)),
        ],
        compiler_params=pltpu.CompilerParams(
            collective_id=collective_id, has_side_effects=True, vmem_limit_bytes=40 * 2**20
        ),
        cost_estimate=lasting(75),
        name=name,
    )(*matrices, gate, up)


def collect_kernel(line_len, *refs):
    grads, (sums_in, columns) = refs[:2], refs[2:4]
    outs, (sums_out, columns_out) = refs[4:6], refs[6:8]
    core_in, chip_in, pair_in, line_in, chip_out, pair_out, line_out = [
        refs[8 + 2 * i : 10 + 2 * i] for i in range(7)
    ]
    sums_got, sums_mine, own_sem = refs[22:25]
    core_sems, chip_sems, pair_sems, line_sems, column_sems, sums_sems = refs[25:]
    b, c = lax.axis_index("batch"), lax.axis_index("ctx")
    n_ctx = 2 * line_len
    line, pair = c // 2, c % 2
    ahead = (b, 2 * lax.rem(line + 1, line_len) + pair)
    across, chip, core = (b, c ^ 1), (b ^ 2, c), (b ^ 1, c)
    others = [(b, lax.rem(c + k, n_ctx)) for k in range(1, n_ctx)]
    on_same_line = others[1::2]
    greet([chip, core] + others)
    keep = pltpu.make_async_copy(columns.at[c], columns_out.at[c], own_sem)
    keep.start()

    def place(index):
        step, side = index // 2, index % 2
        to = lax.rem(line - 1 - step + line_len, line_len)
        return 2 * to + (1 - pair if side == 0 else pair)

    waits = []

    def send(block, target, sems, index, device):
        copy = remote(block, target, sems.at[0, index], sems.at[1, index], device)
        copy.start()
        waits.append(copy)
        return copy

    def start_sums(index, device):
        copy = remote(
            sums_mine, sums_got.at[index], sums_sems.at[0, index], sums_sems.at[1, index], device
        )
        copy.start()
        return copy

    def add_sums(index, copy):
        copy.wait()
        sums_mine[...] += sums_got[index]

    sums_mine[...] = sums_in[...]
    by_core = start_sums(0, core)
    to_core = [[], []]
    for index in range(2 * n_ctx):
        row = b ^ 3 if index < n_ctx else b ^ 1
        for i in range(2):
            to_core[i].append(
                send(
                    grads[i].at[row, place(index % n_ctx)],
                    core_in[i].at[index],
                    core_sems.at[i],
                    index,
                    core,
                )
            )
    add_sums(0, by_core)
    by_chip = start_sums(1, chip)
    on_columns = []
    for k, device in enumerate(others):
        copy = remote(
            columns.at[device[1]],
            columns_out.at[c],
            column_sems.at[0, k],
            column_sems.at[1, k],
            device,
        )
        copy.start()
        on_columns.append(copy)
    to_chip = [[], []]
    for index in range(n_ctx):
        for i in range(2):
            to_core[i][index].wait_recv()
            total = grads[i][b ^ 2, place(index)].astype(F32) + core_in[i][index].astype(F32)
            chip_out[i][index] = total.astype(BF16)
            to_chip[i].append(
                send(chip_out[i].at[index], chip_in[i].at[index], chip_sems.at[i], index, chip)
            )
    add_sums(1, by_chip)
    by_pair = start_sums(2, across)

    def mine(i, index):
        to_core[i][n_ctx + index].wait_recv()
        to_chip[i][index].wait_recv()
        return (
            grads[i][b, place(index)].astype(F32)
            + core_in[i][n_ctx + index].astype(F32)
            + chip_in[i][index].astype(F32)
        )

    to_pair, to_line = [[], []], [[], []]
    for step in range(line_len):
        for i in range(2):
            pair_out[i][step] = mine(i, 2 * step).astype(BF16)
            to_pair[i].append(
                send(pair_out[i].at[step], pair_in[i].at[step], pair_sems.at[i], step, across)
            )
        if step == 0:
            add_sums(2, by_pair)
            own_sums = [
                send(sums_mine, sums_got.at[3 + k], sums_sems, 3 + k, device)
                for k, device in enumerate(on_same_line)
            ]
        for i in range(2):
            total = mine(i, 2 * step + 1)
            to_pair[i][step].wait_recv()
            total = total + pair_in[i][step].astype(F32)
            if step > 0:
                to_line[i][step - 1].wait_recv()
                total = total + line_in[i][step - 1].astype(F32)
            if step < line_len - 1:
                line_out[i][step] = total.astype(BF16)
                to_line[i].append(
                    send(line_out[i].at[step], line_in[i].at[step], line_sems.at[i], step, ahead)
                )
            else:
                outs[i][...] = total
    total = sums_mine[...]
    for k, copy in enumerate(own_sums):
        copy.wait_recv()
        total = total + sums_got[3 + k]
    sums_out[...] = total
    for copy in on_columns:
        copy.wait()
    for copy in waits:
        copy.wait_send()
    keep.wait()


def collect(grads, sums, columns, collective_id, name):
    n_batch, n_ctx = lax.axis_size("batch"), lax.axis_size("ctx")
    line_len = n_ctx // 2
    blocks = [grad.shape[2:] for grad in grads]

    def room(size):
        return [pltpu.VMEM((size,) + block, BF16) for block in blocks]

    return pl.pallas_call(
        functools.partial(collect_kernel, line_len),
        out_shape=(
            *[jax.ShapeDtypeStruct(block, F32) for block in blocks],
            jax.ShapeDtypeStruct(sums.shape, F32),
            jax.ShapeDtypeStruct(columns.shape, BF16),
        ),
        in_specs=[IN_VMEM] * 3 + [ANYWHERE],
        out_specs=(IN_VMEM,) * 3 + (ANYWHERE,),
        scratch_shapes=[
            *room(2 * n_ctx),
            *room(n_ctx),
            *room(line_len),
            *room(line_len - 1),
            *room(n_ctx),
            *room(line_len),
            *room(line_len - 1),
            pltpu.VMEM((2 + line_len,) + sums.shape, F32),
            pltpu.VMEM(sums.shape, F32),
            DMA(()),
            DMA((2, 2, 2 * n_ctx)),
            DMA((2, 2, n_ctx)),
            DMA((2, 2, line_len)),
            DMA((2, 2, line_len)),
            DMA((2, n_ctx)),
            DMA((2, 2 + line_len)),
        ],
        compiler_params=pltpu.CompilerParams(
            collective_id=collective_id, has_side_effects=True, vmem_limit_bytes=60 * 2**20
        ),
        cost_estimate=lasting(70),
        name=name,
    )(*grads, sums, columns)


def row_scale(values):
    return lax.rsqrt(jnp.mean(values * values, axis=-1, keepdims=True) + EPSILON)


def turn_head(values, cosine, signed_sine, back=False):
    turned = pltpu.roll(values, HEAD_DIM // 2, 1) * signed_sine
    return values * cosine - turned if back else values * cosine + turned


def whole(*shape):
    return pl.BlockSpec(shape, lambda j: (0,) * len(shape))


def project_kernel(hidden, gain, weight, bias, cosine, signed_sine, normed, query, key_value, kept):
    j = pl.program_id(0)

    @pl.when(j == 0)
    def _():
        values = hidden[...].astype(F32)
        kept[...] = (values * row_scale(values) * gain[...]).astype(BF16)
        normed[...] = kept[...]

    lin = dot(kept[...], weight[...]) + bias[...]
    tables = cosine[...], signed_sine[...]
    heads = [lin[:, i * HEAD_DIM : (i + 1) * HEAD_DIM] for i in range(4)]

    @pl.when(j < 3)
    def _():
        for i in range(4):
            turned = turn_head(heads[i], *tables)
            query[:, i * HEAD_DIM : (i + 1) * HEAD_DIM] = turned.astype(BF16)

    @pl.when(j == 3)
    def _():
        for i in range(4):
            value = turn_head(heads[i], *tables) if i < KV_HEADS else heads[i]
            key_value[:, i * HEAD_DIM : (i + 1) * HEAD_DIM] = value.astype(BF16)


def project(hidden, gain, weights, bias, tables):
    count, width = hidden.shape
    wide = 2 * KVW
    table = whole(count, HEAD_DIM)
    return pl.pallas_call(
        project_kernel,
        grid=(4,),
        out_shape=(
            jax.ShapeDtypeStruct((count, width), BF16),
            jax.ShapeDtypeStruct((count, width), BF16),
            jax.ShapeDtypeStruct((count, wide), BF16),
        ),
        in_specs=[
            whole(count, width),
            whole(1, width),
            pl.BlockSpec((width, wide), lambda j: (0, j)),
            pl.BlockSpec((1, wide), lambda j: (0, j)),
            table,
            table,
        ],
        out_specs=(
            whole(count, width),
            pl.BlockSpec((count, wide), lambda j: (0, jnp.minimum(j, 2))),
            whole(count, wide),
        ),
        scratch_shapes=[pltpu.VMEM((count, width), BF16)],
        compiler_params=pltpu.CompilerParams(vmem_limit_bytes=40 * 2**20),
        cost_estimate=lasting(4),
        name="project",
    )(hidden, gain, weights, bias, *tables)


def mark_allowed(key_pos, key_doc, own_pos, own_doc, allowed):
    count = own_pos.shape[1]
    pos_column, doc_column = key_pos[...].T, key_doc[...].T
    for i in range(key_pos.shape[0]):
        seen = (pos_column[:, i : i + 1] <= own_pos[...]) & (doc_column[:, i : i + 1] == own_doc[...])
        allowed[i * count : (i + 1) * count] = jnp.where(seen, 1.0, 0.0)


def stack_heads(block, group):
    return jnp.concatenate(
        [block[:, i * HEAD_DIM : (i + 1) * HEAD_DIM] for i in range(group)], axis=0
    )


def lay_heads(stacked, group):
    count = stacked.shape[0] // group
    return jnp.concatenate([stacked[i * count : (i + 1) * count] for i in range(group)], axis=1)


def probabilities(keys, queries, allowed, group):
    scores = times_transposed(keys, queries) * INV_ROOT
    seen = jnp.concatenate([allowed[...]] * group, axis=1) > 0.0
    scores = jnp.where(seen, scores, MASKED)
    raised = jnp.exp(scores - jnp.max(scores, axis=0, keepdims=True))
    return raised * (1.0 / jnp.sum(raised, axis=0, keepdims=True))


def attend_kernel(
    group, last, query, keys, values, out_0, out_1, out_2, key_pos, key_doc, own_pos, own_doc,
    hidden, gain, attn_out, residual, normed, total, allowed,
):
    j = pl.program_id(0)

    @pl.when(j == 0)
    def _():
        total[...] = hidden[...].astype(F32)
        mark_allowed(key_pos, key_doc, own_pos, own_doc, allowed)

    probs = probabilities(keys[...], stack_heads(query[...], group), allowed, group)
    result = contract_rows(values[...], probs.astype(BF16)).T
    block = lay_heads(result, group).astype(BF16)
    attn_out[...] = block
    for t, weight in enumerate((out_0, out_1, out_2)):
        total[:, t * 512 : (t + 1) * 512] += dot(block, weight[...])

    @pl.when(j == last)
    def _():
        values = total[...]
        residual[...] = values
        normed[...] = (values * row_scale(values) * gain[...]).astype(BF16)


def head_specs(count, width, keys, group, weights_at):
    rows = group * HEAD_DIM
    per_key = GROUPS // group
    query = pl.BlockSpec((count, rows), lambda j: (0, j))
    heads = [
        pl.BlockSpec((keys, HEAD_DIM), lambda j, i=i: (0, KV_HEADS * i + j // per_key))
        for i in range(2)
    ]
    out = [
        pl.BlockSpec((rows, 512), lambda j, t=t: (j, weights_at // 512 + t))
        for t in range(width // 512)
    ]
    places = [whole(keys // count, count)] * 2 + [whole(1, count)] * 2
    return query, heads, out, places


def attend(query, key_value, weights, places, hidden, gain):
    count, width = hidden.shape
    keys = key_value.shape[0]
    group = 3 if keys <= 1024 else 1
    steps = HEADS // group
    query_spec, head_spec, out_spec, place_spec = head_specs(
        count, width, keys, group, width + 2 * KVW
    )
    return pl.pallas_call(
        functools.partial(attend_kernel, group, steps - 1),
        grid=(steps,),
        out_shape=(
            jax.ShapeDtypeStruct((count, width), BF16),
            jax.ShapeDtypeStruct((count, width), F32),
            jax.ShapeDtypeStruct((count, width), BF16),
        ),
        in_specs=[query_spec, *head_spec, *out_spec, *place_spec]
        + [whole(count, width), whole(1, width)],
        out_specs=(query_spec, whole(count, width), whole(count, width)),
        scratch_shapes=[pltpu.VMEM((count, width), F32), pltpu.VMEM((keys, count), F32)],
        compiler_params=pltpu.CompilerParams(vmem_limit_bytes=56 * 2**20),
        cost_estimate=lasting(10),
        name="attend",
    )(query, key_value, key_value, *[weights] * 3, *places, hidden, gain)


def attend_back_kernel(
    group, per_key, query, keys, values, out_0, out_1, out_2, key_pos, key_doc, own_pos, own_doc,
    attn_out, residual, gain, out_grad, d_normed, cosine, signed_sine, d_query, d_key_value,
    o_grad, d_residual, gain_grad, branch, allowed, key_sum, value_sum,
):
    j = pl.program_id(0)

    @pl.when(j == 0)
    def _():
        rows, grads = residual[...], d_normed[...]
        factor = row_scale(rows)
        scaled = grads * gain[...]
        gain_grad[...] = jnp.sum(grads * rows * factor, axis=0, keepdims=True)
        total = out_grad[...].astype(F32) + (
            factor * scaled
            - rows * (factor * factor * factor) * jnp.mean(scaled * rows, axis=-1, keepdims=True)
        )
        d_residual[...] = total
        branch[...] = total.astype(BF16)
        mark_allowed(key_pos, key_doc, own_pos, own_doc, allowed)

    @pl.when(lax.rem(j, per_key) == 0)
    def _():
        key_sum[...] = jnp.zeros_like(key_sum)
        value_sum[...] = jnp.zeros_like(value_sum)

    o_grad[...] = contract_rows(attn_out[...], branch[...]).astype(BF16)
    d_attn = sum(
        times_transposed(branch[:, t * 512 : (t + 1) * 512], weight[...])
        for t, weight in enumerate((out_0, out_1, out_2))
    ).astype(BF16)
    grads = stack_heads(d_attn, group)
    queries = stack_heads(query[...], group)
    probs = probabilities(keys[...], queries, allowed, group)
    d_probs = times_transposed(values[...], grads)
    delta = jnp.sum(probs * d_probs, axis=0, keepdims=True)
    d_scores = (probs * (d_probs - delta)).astype(BF16)
    key_sum[...] += dot(d_scores, queries)
    value_sum[...] += dot(probs.astype(BF16), grads)
    result = contract_rows(keys[...], d_scores).T * INV_ROOT
    count = result.shape[0] // group
    for i in range(group):
        head = turn_head(
            result[i * count : (i + 1) * count], cosine[...], signed_sine[...], back=True
        )
        d_query[:, i * HEAD_DIM : (i + 1) * HEAD_DIM] = head.astype(BF16)

    @pl.when(lax.rem(j, per_key) == per_key - 1)
    def _():
        at = pl.multiple_of(j // per_key * HEAD_DIM, HEAD_DIM)
        d_key_value[:, pl.ds(at, HEAD_DIM)] = (key_sum[...] * INV_ROOT).astype(BF16)
        d_key_value[:, pl.ds(KVW + at, HEAD_DIM)] = value_sum[...].astype(BF16)


def attend_back(query, key_value, weights, places, attn_out, residual, gain, out_grad, d_normed, tables):
    count, width = query.shape
    keys = key_value.shape[0]
    group = 3 if keys <= 1024 else 1
    steps = HEADS // group
    query_spec, head_spec, out_spec, place_spec = head_specs(
        count, width, keys, group, width + 2 * KVW
    )
    rows, table = whole(count, width), whole(count, HEAD_DIM)
    return pl.pallas_call(
        functools.partial(attend_back_kernel, group, GROUPS // group),
        grid=(steps,),
        out_shape=(
            jax.ShapeDtypeStruct((count, width), BF16),
            jax.ShapeDtypeStruct((keys, 2 * KVW), BF16),
            jax.ShapeDtypeStruct((width, width), BF16),
            jax.ShapeDtypeStruct((count, width), F32),
            jax.ShapeDtypeStruct((1, width), F32),
        ),
        in_specs=[query_spec, *head_spec, *out_spec, *place_spec, query_spec]
        + [rows, whole(1, width), rows, rows, table, table],
        out_specs=(
            query_spec,
            whole(keys, 2 * KVW),
            pl.BlockSpec((group * HEAD_DIM, width), lambda j: (j, 0)),
            rows,
            whole(1, width),
        ),
        scratch_shapes=[
            pltpu.VMEM((count, width), BF16),
            pltpu.VMEM((keys, count), F32),
            pltpu.VMEM((keys, HEAD_DIM), F32),
            pltpu.VMEM((keys, HEAD_DIM), F32),
        ],
        compiler_params=pltpu.CompilerParams(vmem_limit_bytes=60 * 2**20),
        cost_estimate=lasting(17),
        name="attend_back",
    )(
        query, key_value, key_value, *[weights] * 3, *places, attn_out, residual, gain, out_grad,
        d_normed, *tables,
    )


def project_back_kernel(
    d_query, d_key_value, weight, normed, hidden, gain, d_residual, gain_two_grad, cosine,
    signed_sine, grad, hidden_grad, sums, flipped, total, biases,
):
    j = pl.program_id(0)
    wide = weight.shape[1]

    @pl.when(j == 0)
    def _():
        flipped[...] = normed[...].astype(F32).T.astype(BF16)
        total[...] = jnp.zeros_like(total)
        sums[...] = jnp.zeros_like(sums)

    def add(d_lin):
        grad[...] = dot(flipped[...], d_lin).astype(BF16)
        total[...] += times_transposed(d_lin, weight[...])
        return jnp.sum(d_lin.astype(F32), axis=0, keepdims=True)

    for i in range(3):

        @pl.when(j == i)
        def _():
            sums[1:2, i * wide : (i + 1) * wide] = add(d_query[...])

    @pl.when(j == 3)
    def _():
        heads = [
            turn_head(
                d_key_value[:, i * HEAD_DIM : (i + 1) * HEAD_DIM],
                cosine[...],
                signed_sine[...],
                back=True,
            )
            for i in range(KV_HEADS)
        ]
        d_lin = jnp.concatenate(heads + [d_key_value[:, KVW:]], axis=1).astype(BF16)
        sums[2:3, :wide] = add(d_lin)
        rows, grads = hidden[...].astype(F32), total[...]
        factor = row_scale(rows)
        scaled = grads * gain[...]
        sums[0:1] = jnp.sum(grads * rows * factor, axis=0, keepdims=True)
        sums[3:4] = gain_two_grad[...]
        hidden_grad[...] = d_residual[...] + (
            factor * scaled
            - rows * (factor * factor * factor) * jnp.mean(scaled * rows, axis=-1, keepdims=True)
        )


def project_back(d_query, d_key_value, weights, normed, hidden, gain, d_residual, gain_two_grad, tables):
    count, width = hidden.shape
    wide = 2 * KVW
    rows, table = whole(count, width), whole(count, HEAD_DIM)
    return pl.pallas_call(
        project_back_kernel,
        grid=(4,),
        out_shape=(
            jax.ShapeDtypeStruct((width, width + wide), BF16),
            jax.ShapeDtypeStruct((count, width), F32),
            jax.ShapeDtypeStruct((8, width), F32),
        ),
        in_specs=[
            pl.BlockSpec((count, wide), lambda j: (0, jnp.minimum(j, 2))),
            whole(count, wide),
            pl.BlockSpec((width, wide), lambda j: (0, j)),
            rows,
            rows,
            whole(1, width),
            rows,
            whole(1, width),
            table,
            table,
        ],
        out_specs=(
            pl.BlockSpec((width, wide), lambda j: (0, j)),
            rows,
            whole(8, width),
        ),
        scratch_shapes=[
            pltpu.VMEM((width, count), BF16),
            pltpu.VMEM((count, width), F32),
            pltpu.VMEM((8, wide), F32),
        ],
        compiler_params=pltpu.CompilerParams(vmem_limit_bytes=48 * 2**20),
        cost_estimate=lasting(9),
        name="project_back",
    )(
        d_query, d_key_value, weights, normed, hidden, gain, d_residual, gain_two_grad, *tables
    )


def unpack_kernel(n_batch, piece, packed, gate, up):
    n_ctx, _, both = packed.shape
    for out, first in ((gate, 0), (up, both // 2)):
        for k in range(n_batch):
            for i in range(n_ctx):
                at = first + k * piece
                to = (k * n_ctx + i) * piece
                out[:, to : to + piece] = packed[i, :, at : at + piece].astype(F32)


def unpack(packed, n_batch, width):
    n_ctx, rows, _ = packed.shape
    out = jax.ShapeDtypeStruct((rows, width), F32)
    return pl.pallas_call(
        functools.partial(unpack_kernel, n_batch, width // (n_batch * n_ctx)),
        out_shape=(out, out),
        in_specs=[IN_VMEM],
        out_specs=(IN_VMEM, IN_VMEM),
        compiler_params=pltpu.CompilerParams(vmem_limit_bytes=40 * 2**20),
        cost_estimate=lasting(3),
        name="unpack",
    )(packed)


def mlp_kernel(
    line_len, tile, own_rows, *refs
):
    n_batch, n_ctx = 4, 2 * line_len
    weights, (down, grads_in) = refs[:n_batch], refs[n_batch : n_batch + 2]
    total_out, ff_out, down_out = refs[n_batch + 2 : n_batch + 5]
    grad_outs = refs[n_batch + 5 : 2 * n_batch + 5]
    (
        tokens, gate_up, down_in, grads, mixed, d_gate_up, parts, pair_in, line_in, line_out,
        ff_part, gate_up_grad, down_grad, own, load_sems, store_sems, line_sems, pair_sems,
        back_pair, back_line,
    ) = refs[2 * n_batch + 5 :]
    b, c = lax.axis_index("batch"), lax.axis_index("ctx")
    line, pair = c // 2, c % 2
    ahead = (b, 2 * lax.rem(line + 1, line_len) + pair)
    behind = (b, 2 * lax.rem(line + line_len - 1, line_len) + pair)
    across = (b, c ^ 1)
    count, width = own.shape
    half = gate_up.shape[1] // 2
    own_ff = down.shape[0]
    depth = width // n_batch
    for k in range(n_batch):
        source = pl.ds(pl.multiple_of((b ^ k) * depth, 128), depth)
        own[:, k * depth : (k + 1) * depth] = own_rows[:, source]
    greet((ahead, behind, across))

    def at(step):
        return 2 * lax.rem(line - step + line_len, line_len)

    on_line, on_pair, on_back, on_passed = [], [], [], []

    def forward(step):
        block = own if step == 0 else tokens.at[at(step) + pair]
        target = tokens.at[at(step) + pair]
        if step > 0:
            on_line[step - 1].wait_recv()
        if step < line_len - 1:
            copy = remote(block, target, line_sems.at[0, step], line_sems.at[1, step], ahead)
            copy.start()
            on_line.append(copy)
        copy = remote(block, target, pair_sems.at[0, step], pair_sems.at[1, step], across)
        copy.start()
        on_pair.append(copy)

    forward(0)
    loads = [pltpu.make_async_copy(own, tokens.at[c], load_sems.at[0])]
    for k, weight in enumerate(weights):
        loads.append(
            pltpu.make_async_copy(
                weight, gate_up.at[pl.ds(k * depth, depth)], load_sems.at[1 + k]
            )
        )
    loads.append(
        pltpu.make_async_copy(down, down_in.at[pl.ds(0, own_ff)], load_sems.at[1 + n_batch])
    )
    loads.append(pltpu.make_async_copy(grads_in, grads, load_sems.at[2 + n_batch]))
    for copy in loads:
        copy.start()
    if own_ff < half:
        down_in[own_ff:half] = jnp.zeros((half - own_ff, width), BF16)
    for copy in loads:
        copy.wait()

    def chunk(step):
        first = pl.multiple_of(at(step) * count, 2 * count)
        rows = pl.ds(first, 2 * count)
        block = tokens[pl.ds(at(step), 2)].reshape(2 * count, width)
        grad_block = grads[pl.ds(at(step), 2)].reshape(2 * count, width)

        def columns(index, _):
            low = pl.multiple_of(index * tile, 128)
            high = pl.multiple_of(half + index * tile, 128)
            gate_lin = dot(block, gate_up[:, pl.ds(low, tile)])
            up_lin = dot(block, gate_up[:, pl.ds(high, tile)])
            d_mixed = times_transposed(grad_block, down_in[pl.ds(low, tile)])
            sigmoid = 1.0 / (1.0 + jnp.exp(-gate_lin))
            silu = gate_lin * sigmoid
            mixed[rows, pl.ds(low, tile)] = (silu * up_lin).astype(BF16)
            d_gate = d_mixed * up_lin * sigmoid * (1.0 + gate_lin * (1.0 - sigmoid))
            d_gate_up[rows, pl.ds(low, tile)] = d_gate.astype(BF16)
            d_gate_up[rows, pl.ds(high, tile)] = (d_mixed * silu).astype(BF16)
            return 0

        lax.fori_loop(0, half // tile, columns, 0)

        def features(index, _):
            low = pl.multiple_of(index * depth, 128)
            back = times_transposed(d_gate_up[rows], gate_up[pl.ds(low, depth)])
            parts[pl.ds(at(step), 2), :, pl.ds(low, depth)] = back.astype(BF16).reshape(
                2, count, depth
            )
            return 0

        lax.fori_loop(0, n_batch, features, 0)

    def give(step):
        index = (step + line_len - 1) % line_len
        copy = remote(
            parts.at[at(step) + 1 - pair],
            pair_in.at[index],
            back_pair.at[0, index],
            back_pair.at[1, index],
            across,
        )
        copy.start()
        on_back.append(copy)

    for step in range(line_len):
        if step + 1 < line_len:
            forward(step + 1)
        on_pair[step].wait_recv()
        chunk(step)
        if step > 0:
            give(step)
    give(0)

    def passing(index):
        on_back[index].wait_recv()
        total = parts[at(index + 1) + pair].astype(F32) + pair_in[index].astype(F32)
        if index > 0:
            on_passed[index - 1].wait_recv()
            total = total + line_in[index - 1].astype(F32)
        if index < line_len - 1:
            line_out[index] = total.astype(BF16)
            copy = remote(
                line_out.at[index],
                line_in.at[index],
                back_line.at[0, index],
                back_line.at[1, index],
                ahead,
            )
            copy.start()
            on_passed.append(copy)
        else:
            for k in range(n_batch):
                target = pl.ds(pl.multiple_of((b ^ k) * depth, 128), depth)
                total_out[:, target] = total[:, k * depth : (k + 1) * depth]

    stores = []

    def store(source, target):
        copy = pltpu.make_async_copy(source, target, store_sems.at[len(stores)])
        copy.start()
        stores.append(copy)

    def weight_grad(k):
        block = tokens[:, :, k * depth : (k + 1) * depth].reshape(n_ctx * count, depth)

        def columns(index, _):
            low = pl.multiple_of(index * tile, 128)
            grad = contract_rows(block, d_gate_up[:, pl.ds(low, tile)])
            gate_up_grad[k, :, pl.ds(low, tile)] = grad.astype(BF16)
            return 0

        lax.fori_loop(0, 2 * half // tile, columns, 0)
        store(gate_up_grad.at[k], grad_outs[k])

    def down_grads():
        def columns(index, _):
            low = pl.multiple_of(index * tile, 128)
            grad = contract_rows(
                mixed[:, pl.ds(low, tile)], grads[...].reshape(n_ctx * count, width)
            )
            down_grad[pl.ds(low, tile)] = grad.astype(BF16)
            return 0

        lax.fori_loop(0, half // tile, columns, 0)
        store(down_grad.at[pl.ds(0, own_ff)], down_out)

    def ff_parts():
        def rows(index, _):
            low = pl.multiple_of(index * 2 * count, 2 * count)
            out = dot(mixed[pl.ds(low, 2 * count)], down_in[...])
            ff_part[pl.ds(low, 2 * count)] = out.astype(BF16)
            return 0

        lax.fori_loop(0, line_len, rows, 0)
        store(ff_part, ff_out)

    work = [
        lambda: (weight_grad(1), weight_grad(3)),
        lambda: (weight_grad(2), weight_grad(0)),
        down_grads,
        ff_parts,
    ]
    for index in range(max(line_len, len(work))):
        if index < len(work):
            work[index]()
        if index < line_len:
            passing(index)
    for copy in on_line + on_pair + on_back + on_passed:
        copy.wait_send()
    for copy in stores:
        copy.wait()


def mlp_scratch(n_ctx, n_batch, count, width, half):
    line_len = n_ctx // 2

    def room(*shape):
        return pltpu.VMEM(shape, BF16)

    return [
        room(n_ctx, count, width),
        room(width, 2 * half),
        room(half, width),
        room(n_ctx, count, width),
        room(n_ctx * count, half),
        room(n_ctx * count, 2 * half),
        room(n_ctx, count, width),
        room(line_len, count, width),
        room(line_len - 1, count, width),
        room(line_len - 1, count, width),
        room(n_ctx * count, width),
        room(n_batch, width // n_batch, 2 * half),
        room(half, width),
        room(count, width),
    ]


def mlp(own, weights, down, grads, collective_id, name):
    n_batch, n_ctx = lax.axis_size("batch"), lax.axis_size("ctx")
    line_len = n_ctx // 2
    count, width = own.shape
    half = weights[0].shape[1] // 2
    depth = width // n_batch
    tile = 384 if half % 384 == 0 else 128
    return pl.pallas_call(
        functools.partial(mlp_kernel, line_len, tile),
        out_shape=(
            jax.ShapeDtypeStruct((count, width), F32),
            jax.ShapeDtypeStruct((n_ctx * count, width), BF16),
            jax.ShapeDtypeStruct(down.shape, BF16),
            *[jax.ShapeDtypeStruct((depth, 2 * half), BF16)] * n_batch,
        ),
        in_specs=[IN_VMEM] + [ANYWHERE] * (n_batch + 2),
        out_specs=(IN_VMEM,) + (ANYWHERE,) * (n_batch + 2),
        scratch_shapes=mlp_scratch(n_ctx, n_batch, count, width, half)
        + [
            DMA((3 + n_batch,)),
            DMA((2 + n_batch,)),
            DMA((2, line_len)),
            DMA((2, line_len)),
            DMA((2, line_len)),
            DMA((2, line_len)),
        ],
        compiler_params=pltpu.CompilerParams(
            collective_id=collective_id, has_side_effects=True, vmem_limit_bytes=60 * 2**20
        ),
        cost_estimate=lasting(90),
        name=name,
    )(own, *weights, down, grads.reshape(n_ctx, count, width))


def swap(values, bit):
    size = lax.axis_size("batch")
    return lax.ppermute(values, "batch", [(i, i ^ bit) for i in range(size)])


def by_batch(values, b, n_batch):
    step = values.shape[1] // n_batch
    blocks = [lax.dynamic_slice_in_dim(values, (b ^ k) * step, step, 1) for k in range(n_batch)]
    return jnp.concatenate(blocks, axis=1)


def half_sum(terms):
    passed = swap((terms[2].astype(F32) + swap(terms[3], 1).astype(F32)).astype(BF16), 2)
    return terms[0], swap(terms[1], 1), passed


def mlp_room(n_ctx, n_batch, count, width, half):
    return sum(math.prod(room.shape) for room in mlp_scratch(n_ctx, n_batch, count, width, half))


def mlp_in_steps(normed_two, w_gate_up, w_down, out_grad_all):
    n_ctx = lax.axis_size("ctx")
    w_gate_up = jnp.concatenate(w_gate_up, axis=0)
    half, width = w_gate_up.shape[1] // 2, normed_two.shape[1]
    own_ff = w_down.shape[0]
    w_down = jnp.pad(w_down, ((0, half - own_ff), (0, 0)))
    normed_two = gather_ctx(normed_two, 3, "gather_tokens").reshape(-1, width)
    gate_up = dot(normed_two, w_gate_up)
    gate_lin, up_lin = gate_up[:, :half], gate_up[:, half:]
    sigmoid_gate = jax.nn.sigmoid(gate_lin)
    mixed_rows = (gate_lin * sigmoid_gate * up_lin).astype(BF16)
    d_mixed = times_transposed(out_grad_all, w_down)
    d_gate = d_mixed * up_lin * sigmoid_gate * (1.0 + gate_lin * (1.0 - sigmoid_gate))
    d_up = d_mixed * (gate_lin * sigmoid_gate)
    d_gate_up = jnp.concatenate([d_gate.astype(BF16), d_up.astype(BF16)], axis=1)
    (d_normed_two,) = scatter_ctx(
        [times_transposed(d_gate_up, w_gate_up).astype(BF16)], 4, "scatter_tokens"
    )
    grads = contract_rows(normed_two, d_gate_up).astype(BF16).reshape(4, -1, 2 * half)
    return (
        d_normed_two,
        dot(mixed_rows, w_down).astype(BF16),
        contract_rows(mixed_rows, out_grad_all).astype(BF16)[:own_ff],
        *grads,
    )


def vector_rows(vectors, rows, pieces):
    laid = [
        jnp.pad(v.reshape(pieces, 1, -1), ((0, 0), (0, 0), (0, 128 - v.shape[0] // pieces)))
        for v in vectors
    ]
    return jnp.pad(jnp.concatenate(laid, axis=1), ((0, 0), (0, rows - len(vectors)), (0, 0)))


def local(
    hidden_in,
    positions,
    doc_ids,
    attn_gain,
    q_weight,
    q_bias,
    k_weight,
    k_bias,
    v_weight,
    v_bias,
    o_weight,
    mlp_gain,
    gate_weight,
    up_weight,
    down_weight,
    out_grad,
):
    n_batch, n_ctx = lax.axis_size("batch"), lax.axis_size("ctx")
    n_all = n_batch * n_ctx
    count, width = hidden_in.shape
    hidden_ff = gate_weight.shape[1]

    b = lax.axis_index("batch")
    w_down = lax.all_gather(down_weight, "batch", axis=0, tiled=True)
    out_grad_all = lax.all_gather(out_grad, "ctx", axis=0, tiled=True)
    rows = q_weight.shape[0]
    small = (attn_gain, mlp_gain, q_bias, k_bias, v_bias)
    places = (positions // 64, positions % 64, doc_ids)
    small = vector_rows(small + tuple(row.astype(BF16) for row in places), rows, 1)[0]
    matrices = (q_weight, k_weight, v_weight, o_weight, small)
    attn_all, packed = spread(matrices, gate_weight, up_weight, 1, "spread_weights")
    half = packed.shape[2] // 2
    own_rows = packed.reshape(-1, 2 * half)
    near, far = swap(own_rows, 1), swap(own_rows, 2)
    small = attn_all[:, :, :8, attn_all.shape[3] - 128 :].astype(F32)
    gain_one, gain_two, b_query, b_key, b_value = (
        small[:, :, i, : part.shape[0]].reshape(-1)
        for i, part in enumerate((attn_gain, mlp_gain, q_bias, k_bias, v_bias))
    )
    places = lax.dynamic_index_in_dim(small, b, 0, keepdims=False)[:, 5:8, :count]
    key_pos, key_doc = places[:, 0] * 64 + places[:, 1], places[:, 2]
    attn_all = attn_all.reshape(width, -1)
    b_qkv = jnp.concatenate([b_query, b_key, b_value])

    cosine, sine_table = rope_tables(positions)
    half_lane = jnp.arange(HEAD_DIM) < HEAD_DIM // 2
    tables = cosine, jnp.where(half_lane[None], -sine_table, sine_table)
    normed_one, query, key_value = project(hidden_in, gain_one[None], attn_all, b_qkv[None], tables)
    key_value = gather_ctx(key_value, 2, "gather_keys").reshape(-1, 2 * KVW)
    far, key_value = lax.optimization_barrier((far, key_value))
    w_gate_up = (own_rows, near, far, swap(far, 1))
    places = (
        key_pos, key_doc, positions.astype(F32)[None], doc_ids.astype(F32)[None]
    )
    attn_out, residual, normed_two = attend(
        query, key_value, attn_all, places, hidden_in, gain_two[None]
    )

    fused = 2 * mlp_room(n_ctx, n_batch, count, width, half) < 52 * 2**20
    d_normed_two, ff_out, down_terms, *gate_up_terms = (
        mlp(normed_two, w_gate_up, w_down, out_grad_all, 3, "mlp")
        if fused
        else mlp_in_steps(by_batch(normed_two, b, n_batch), w_gate_up, w_down, out_grad_all)
    )
    if not fused:
        d_normed_two = by_batch(d_normed_two, b, n_batch)
    gate_up_sum = half_sum(gate_up_terms)
    down_terms = down_terms.reshape(n_batch, -1, width)
    down_sum = half_sum(
        [lax.dynamic_index_in_dim(down_terms, b ^ k, 0, False) for k in range(n_batch)]
    )

    d_query, d_key_value, o_grad, d_residual, gain_two_grad = attend_back(
        query, key_value, attn_all, places, attn_out, residual, gain_two[None], out_grad,
        d_normed_two, tables,
    )
    d_key_value, ff_out = scatter_ctx([d_key_value, ff_out], 5, "scatter_rows")
    hidden_out = (residual + ff_out).astype(BF16)
    d_key_value, down_sum, gate_up_sum = lax.optimization_barrier(
        (d_key_value, down_sum, gate_up_sum)
    )
    down_grad = sum(term.astype(F32) for term in down_sum)
    gate_up_grad = sum(term.astype(F32) for term in gate_up_sum).astype(BF16)
    qkv_grad, hidden_grad, sums = project_back(
        d_query, d_key_value, attn_all, normed_one, hidden_in, gain_one[None], d_residual,
        gain_two_grad, tables,
    )
    grads = [grad.reshape(n_batch, n_ctx, rows, -1) for grad in (qkv_grad, o_grad)]
    attn_grads, o_grad, sums, gate_up_grad = collect(
        grads, sums, gate_up_grad.reshape(n_ctx, rows, 2 * half), 6, "collect"
    )
    gate_grad, up_grad = unpack(gate_up_grad, n_batch, hidden_ff)

    def own_part(row, first, total):
        size = total // n_all
        at = first + (b * n_ctx + lax.axis_index("ctx")) * size
        return lax.dynamic_slice(sums, (row, at), (1, size))[0]

    at_key, at_value, at_out = width, width + KVW, width + 2 * KVW
    return (
        hidden_out,
        hidden_grad,
        own_part(0, 0, width),
        attn_grads[:, :at_key],
        own_part(1, 0, width),
        attn_grads[:, at_key:at_value],
        own_part(2, 0, KVW),
        attn_grads[:, at_value:at_out],
        own_part(2, KVW, KVW),
        o_grad,
        own_part(3, 0, width),
        gate_grad,
        up_grad,
        down_grad,
    )


def solution(mesh):
    matrix, vector = P(ALL, None), P(ALL)
    placed = (
        (matrix, vector, vector, vector, matrix, vector, matrix, vector)
        + (matrix, vector, matrix, vector, matrix, matrix, matrix, matrix)
    )
    results = (matrix, matrix) + (vector, matrix) * 4 + (vector, matrix, matrix, matrix)
    return jax.shard_map(local, mesh=mesh, in_specs=placed, out_specs=results, check_vma=False)
```

time: 559 us -> 445 us (0.80); the launches traced: 550 us -> 444 us
  matrix products: 100 us -> 0 us
  Pallas kernels: 312 us -> 381 us
  local copies, waits for them, and re-layouts: 68 us -> 26.7 us
  other arithmetic: 49.8 us -> 17.4 us
    pallas_call x3 -> x8, Pallas kernels: 157 us -> 262 us  [the longest x1 92.1 us: mlp(): pl.pallas_call(functools.partial(mlp_kernel, line_len, tile), out_shape=(...]
    dot_general x17 -> x0, matrix products: 95.5 us -> none  [the longest x4 34.3 us: times_transposed(): lax.dot_general(lhs, rhs, (((1,), (1,)), ((), ())), preferred_element_typ...]
    pallas_call x2 -> x1, Pallas kernels: 79.5 us -> 32.7 us  [gather_ctx(): pl.pallas_call(functools.partial(gather_kernel, line_len), out_shape=jax....]
    reshape x16 -> x0, local copies, waits for them, and re-layouts: 24.3 us -> none  [the longest x4 8.07 us: pack_columns(): packed = weight.reshape(rows, n_batch, n_ctx, piece).transpose(2, 0, 1, 3)]
    concatenate x7 -> x0, other arithmetic: 16.1 us -> none  [the longest x1 9.68 us: local(): jnp.concatenate([qkv_grad.astype(BF16).reshape(n_all, rows, -1), out_proj...]
    convert_element_type x11 -> x5, other arithmetic: 22.4 us -> 11.2 us  [the longest x2 4.17 us: half_sum(): (terms[2].astype(F32) + swap(terms[3], 1).astype(F32)).astype(BF16)]
    pallas_call x1, Pallas kernels: 76.2 us -> 85.6 us  [spread(): pl.pallas_call(functools.partial(spread_kernel, line_len), out_shape=(jax...]
    slice x17 -> x1, local copies, waits for them, and re-layouts: 9.71 us -> 1.7 us  [local(): attn_grads[:, :at_key]]
  transfers between devices with their start and end apart: 10 -> 11, of which waited for: 0 -> 1; matrix products, arithmetic and copies ran while one was open for 19% -> 4% of each run, Pallas kernels for 39% -> 45%
where the time goes in v3:
time: 445 us; the launch traced here: 444 us
  Pallas kernels  381 us (86%)
  local copies, waits for them, and re-layouts  26.7 us (6%)
  other arithmetic  17.4 us (4%)
  between operations  14.5 us (3%)
    pallas_call x1, Pallas kernels, mlp(): pl.pallas_call(functools.partial(mlp_kernel, line_len, tile), out_shape=(...  92.1 us
    pallas_call x1, Pallas kernels, spread(): pl.pallas_call(functools.partial(spread_kernel, line_len), out_shape=(jax...  85.6 us
    pallas_call x1, Pallas kernels, collect(): pl.pallas_call(functools.partial(collect_kernel, line_len), out_shape=(*[...  75.6 us
    pallas_call x1, Pallas kernels, scatter_ctx(): pl.pallas_call(functools.partial(scatter_kernel, line_len, many), out_sha...  55.1 us
    pallas_call x1, Pallas kernels, gather_ctx(): pl.pallas_call(functools.partial(gather_kernel, line_len), out_shape=jax....  32.7 us
    pallas_call x1, Pallas kernels, attend_back(): pl.pallas_call(functools.partial(attend_back_kernel, group, GROUPS // gro...  16.2 us
    unnamed x53, local copies, waits for them, and re-layouts  13 us
    pallas_call x1, Pallas kernels, attend(): pl.pallas_call(functools.partial(attend_kernel, group, steps - 1), grid=(...  9.59 us
  transfers between devices with their start and end apart: 11, of which 1 were waited for; matrix products, arithmetic and copies ran while one was open for 4% of the time, Pallas kernels for 45%

profile of v3, /device:TPU:0, one launch (start us, length us, event | category | flops | bytes accessed | tf_op | source)
XLA Modules:
  0.0 444.2 jit_solution(1867091860809243577)
XLA Ops:
  13.2 1.2 convert_bitcast_fusion
  19.0 85.6 %spread_weights.1 = (bf16[4,8,48,3712]{3,2,1,0:T(8,128)(2,1)}, bf16[8,48,2304]{2,1,0:T(8,128)(2,1)S(1)}) custom-call(bf16[48,1536]{1,0:T(8,128)(2,1)S(1)} %copy-done.15, bf16[48,256]{1,0:T(8,128)(2,1)S(1)} %copy-done.19, bf16[48,256]{1,0:T(8,128)(2,1)S(1)} %copy-done.20, bf16[48,1536]{1,0:T(8,128)(2,1)S(1)} %copy-done.16, ...), custom_call_target="tpu_custom_call" | custom-call | bytes 247500000 | tf_op jit(solution)/shard_map/spread_weights/pallas_call | solution.py:287
  107.1 4.3 copy-done
  111.4 2.9 project.1
  115.7 32.7 %gather_keys.1 = bf16[8,128,512]{2,1,0:T(8,128)(2,1)} custom-call(bf16[128,512]{1,0:T(8,128)(2,1)} %copy-done.17), custom_call_target="tpu_custom_call" | custom-call | bytes 66000000 | tf_op jit(solution)/shard_map/gather_keys/pallas_call | solution.py:109
  149.9 9.6 %attend.1 = (bf16[128,1536]{1,0:T(8,128)(2,1)}, f32[128,1536]{1,0:T(8,128)}, bf16[128,1536]{1,0:T(8,128)(2,1)}) custom-call(bf16[128,1536]{1,0:T(8,128)(2,1)} %copy-done.5, bf16[1024,512]{1,0:T(8,128)(2,1)} %bitcast.66, bf16[1024,512]{1,0:T(8,128)(2,1)} %bitcast.67, bf16[1536,3712]{1,0:T(8,128)(2,1)} %bitcast.54, bf16[1536,3712]{1,0:T(8,128)(2,1)} %bitcast.55, ...), custom_call_target="tpu_custom_call" | custom-call | bytes 33000000 | tf_op jit(solution)/shard_map/attend/pallas_call | solution.py:634
  159.5 92.1 %mlp.1 = (f32[128,1536]{1,0:T(8,128)}, bf16[1024,1536]{1,0:T(8,128)(2,1)}, bf16[1120,1536]{1,0:T(8,128)(2,1)}, bf16[384,2304]{1,0:T(8,128)(2,1)}, bf16[384,2304]...) custom-call(bf16[128,1536]{1,0:T(8,128)(2,1)} %get-tuple-element.61.own_rows, ...), custom_call_target="tpu_custom_call" | custom-call | bytes 297000000 | tf_op jit(solution)/shard_map/mlp/pallas_call | solution.py:1090
  251.7 3.2 dynamic-slice_bitcast_fusion
  255.6 1.6 add_convert_fusion.1
  257.3 1.3 collective-permute-start.8
  258.6 2.5 fusion
  261.9 16.2 %attend_back.1 = (bf16[128,1536]{1,0:T(8,128)(2,1)}, bf16[1024,512]{1,0:T(8,128)(2,1)}, bf16[1536,1536]{1,0:T(8,128)(2,1)}, f32[128,1536]{1,0:T(8,128)}, f32[1,1536]{1,0:T(1,128)}) custom-call(bf16[128,1536]{1,0:T(8,128)(2,1)} %copy-done.5, bf16[1024,512]{1,0:T(8,128)(2,1)} %bitcast.68, bf16[1024,512]{1,0:T(8,128)(2,1)} %bitcast.69, ...), custom_call_target="tpu_custom_call" | custom-call | bytes 56100000 | tf_op jit(solution)/shard_map/attend_back/pallas_call | solution.py:715
  278.1 55.1 %scatter_rows.1 = (f32[128,512]{1,0:T(8,128)}, f32[128,1536]{1,0:T(8,128)}) custom-call(bf16[8,128,512]{2,1,0:T(8,128)(2,1)} %bitcast.77, bf16[8,128,1536]{2,1,0:T(8,128)(2,1)} %bitcast.75), custom_call_target="tpu_custom_call" | custom-call | bytes 132000000 | tf_op jit(solution)/shard_map/scatter_rows/pallas_call | solution.py:179
  333.2 2.1 add_convert_fusion.2
  335.4 4.0 add_convert_fusion
  339.4 8.6 %project_back.1 = (bf16[1536,2048]{1,0:T(8,128)(2,1)}, f32[128,1536]{1,0:T(8,128)}, f32[8,1536]{1,0:T(8,128)S(1)}) custom-call(bf16[128,1536]{1,0:T(8,128)(2,1)S(1)} %copy-done.13, f32[128,512]{1,0:T(8,128)S(1)} %copy-done.14, bf16[1536,3712]{1,0:T(8,128)(2,1)} %bitcast.60, bf16[128,1536]{1,0:T(8,128)(2,1)S(1)} %get-tuple-element.75.normed, ...), custom_call_target="tpu_custom_call" | custom-call | bytes 29700000 | tf_op jit(solution)/shard_map/project_back/pallas_call | solution.py:801
  348.6 75.6 %collect.1 = (f32[48,2048]{1,0:T(8,128)}, f32[48,1536]{1,0:T(8,128)}, f32[8,1536]{1,0:T(8,128)}, bf16[8,48,2304]{2,1,0:T(8,128)(2,1)}) custom-call(bf16[4,8,48,2048]{3,2,1,0:T(8,128)(2,1)} %bitcast.71, bf16[4,8,48,1536]{3,2,1,0:T(8,128)(2,1)} %bitcast.72, f32[8,1536]{1,0:T(8,128)} %copy-done.18, bf16[8,48,2304]{2,1,0:T(8,128)(2,1)} %bitcast.70), custom_call_target="tpu_custom_call" | custom-call | bytes 231000000 | tf_op jit(solution)/shard_map/collect/pallas_call | solution.py:452
  424.3 1.7 slice.49
  426.0 1.5 fusion.6
  427.4 1.5 copy-done.3
  428.9 2.3 unpack.1
  431.3 1.4 dynamic-slice_bitcast_fusion.3
  432.7 1.3 dynamic-slice_bitcast_fusion.4
  433.9 2.7 convert_add_fusion.1
  (98 shorter events, 18.6 us)
Async XLA Ops:
  7.2 7.3 %copy-start.10 = (bf16[48,8960]{1,0:T(8,128)(2,1)S(1)}, bf16[48,8960]{1,0:T(8,128)(2,1)}, u32[]{:S(2)}) copy-start(bf16[48,8960]{1,0:T(8,128)(2,1)} %gate.1) | copy-start | bytes 2580484
  7.2 152.3 %all-gather.3.cloned.1.call-start = ((), (), s32[]{:S(2)}) async-start(), calls=%async_computation | async-start | bytes 4300800 | tf_op jit(solution)/shard_map/all_gather | solution.py:1196
  7.9 99.2 %copy-start.1 = (bf16[128,1536]{1,0:T(8,128)(2,1)S(1)}, bf16[128,1536]{1,0:T(8,128)(2,1)}, u32[]{:S(2)}) copy-start(bf16[128,1536]{1,0:T(8,128)(2,1)} %hidden.5) | copy-start | bytes 1179652
  7.9 151.6 %all-gather.5.cloned.1.call-start = ((), (), s32[]{:S(2)}) async-start(), calls=%async_computation.1 | async-start | bytes 3538944 | tf_op jit(solution)/shard_map/all_gather | solution.py:1197
  104.6 9.7 %copy-start.4 = (bf16[8,48,2304]{2,1,0:T(8,128)(2,1)}, bf16[8,48,2304]{2,1,0:T(8,128)(2,1)S(1)}, u32[]{:S(2)}) copy-start(bf16[8,48,2304]{2,1,0:T(8,128)(2,1)S(1)} %get-tuple-element.56) | copy-start | bytes 5308420
  104.6 43.9 %collective-permute-start = (bf16[384,2304]{1,0:T(8,128)(2,1)S(1)}, bf16[384,2304]{1,0:T(8,128)(2,1)}, u32[]{:S(2)}, u32[]{:S(2)}) collective-permute-start(bf16[384,2304]{1,0:T(8,128)(2,1)S(1)} %bitcast.62), channel_id=1, source_target_pairs={{0,16},{8,24},{16,0},{24,8},{1,17},{9,25},{17,1},{25,9},{2,18},{10... | collective-permute-start | bytes 5308424 | tf_op jit(solution)/shard_map/ppermute | solution.py:1119
  105.0 54.5 %collective-permute-start.1 = (bf16[384,2304]{1,0:T(8,128)(2,1)S(1)}, bf16[384,2304]{1,0:T(8,128)(2,1)}, u32[]{:S(2)}, u32[]{:S(2)}) collective-permute-start(bf16[384,2304]{1,0:T(8,128)(2,1)S(1)} %bitcast.63), channel_id=1, source_target_pairs={{0,8},{8,0},{16,24},{24,16},{1,9},{9,1},{17,25},{25,17},{2,10},{10... | collective-permute-start | bytes 5308424 | tf_op jit(solution)/shard_map/ppermute | solution.py:1119
  107.1 7.2 %copy-start.6 = (f32[128,128]{1,0:T(8,128)}, f32[128,128]{1,0:T(8,128)S(1)}, u32[]{:S(2)}) copy-start(f32[128,128]{1,0:T(8,128)S(1)} %get-tuple-element.104.signed_sine) | copy-start | bytes 196612
  107.1 7.2 %copy-start.8 = (f32[128,128]{1,0:T(8,128)}, f32[128,128]{1,0:T(8,128)S(1)}, u32[]{:S(2)}) copy-start(f32[128,128]{1,0:T(8,128)S(1)} %get-tuple-element.105.cosine) | copy-start | bytes 196612
  107.1 4.3 copy-start
  148.5 11.0 %collective-permute-start.2 = (bf16[384,2304]{1,0:T(8,128)(2,1)}, bf16[384,2304]{1,0:T(8,128)(2,1)}, u32[]{:S(2)}, u32[]{:S(2)}) collective-permute-start(bf16[384,2304]{1,0:T(8,128)(2,1)} %collective-permute-done.refs_2_), channel_id=1, source_target_pairs={{0,8},{8,0},{16,24},{24,16},{1,9},{9,1},{17,25},{25,17},{2,10},{10... | collective-permute-start | bytes 5308424 | tf_op jit(solution)/shard_map/ppermute | solution.py:1119
  251.6 4.0 collective-permute-start.7
  254.9 3.7 collective-permute-start.4
  255.4 79.9 %collective-permute-start.6 = (bf16[384,2304]{1,0:T(8,128)(2,1)}, bf16[384,2304]{1,0:T(8,128)(2,1)}, u32[]{:S(2)}, u32[]{:S(2)}) collective-permute-start(bf16[384,2304]{1,0:T(8,128)(2,1)} %get-tuple-element.71), channel_id=1, source_target_pairs={{0,8},{8,0},{16,24},{24,16},{1,9},{9,1},{17,25},{25,17},{2,10},{10... | collective-permute-start | bytes 5308424 | tf_op jit(solution)/shard_map/ppermute | solution.py:1119
  257.3 78.1 %collective-permute-start.8 = (bf16[384,2304]{1,0:T(8,128)(2,1)}, bf16[384,2304]{1,0:T(8,128)(2,1)}, u32[]{:S(2)}, u32[]{:S(2)}) collective-permute-start(bf16[384,2304]{1,0:T(8,128)(2,1)} %add_convert_fusion.1), channel_id=1, source_target_pairs={{0,16},{8,24},{16,0},{24,8},{1,17},{9,25},{17,1},{25,9},{2,18},{10... | collective-permute-start | bytes 5308424 | tf_op jit(solution)/shard_map/ppermute | solution.py:1119
  258.6 76.7 %collective-permute-start.3 = (bf16[280,1536]{1,0:T(8,128)(2,1)}, bf16[280,1536]{1,0:T(8,128)(2,1)S(1)}, u32[]{:S(2)}, u32[]{:S(2)}) collective-permute-start(bf16[280,1536]{1,0:T(8,128)(2,1)} %get-tuple-element.100), channel_id=1, source_target_pairs={{0,8},{8,0},{16,24},{24,16},{1,9},{9,1},{17,25},{25,17},{2,10},{10... | collective-permute-start | bytes 2580488 | tf_op jit(solution)/shard_map/ppermute | solution.py:1119
  261.2 74.2 %collective-permute-start.5 = (bf16[280,1536]{1,0:T(8,128)(2,1)}, bf16[280,1536]{1,0:T(8,128)(2,1)}, u32[]{:S(2)}, u32[]{:S(2)}) collective-permute-start(bf16[280,1536]{1,0:T(8,128)(2,1)} %fusion), channel_id=1, source_target_pairs={{0,16},{8,24},{16,0},{24,8},{1,17},{9,25},{17,1},{25,9},{2,18},{10... | collective-permute-start | bytes 2580488 | tf_op jit(solution)/shard_map/ppermute | solution.py:1119
  278.1 55.1 %copy-start.22 = (f32[128,1536]{1,0:T(8,128)S(1)}, f32[128,1536]{1,0:T(8,128)}, u32[]{:S(2)}) copy-start(f32[128,1536]{1,0:T(8,128)} %get-tuple-element.59.residual) | copy-start | bytes 2359300
  335.4 4.0 copy-start.2
  335.4 4.0 copy-start.7
  335.4 4.0 copy-start.9
  335.4 4.0 copy-start.12
  335.4 4.0 copy-start.13
  335.4 4.0 copy-start.14
  (13 other events, 20.7 us)
Sparse Core Ops, SparseCore 0:
  9.6 46.7 all-gather.2
  58.5 85.0 all-gather.4
